TPU v7x, 512 devices: a whole 4x4x16 slice. The times are simulated.
512 devices in a mesh: section: 8 (over z_hi, x), expert: 64 (over y, z_lo, core).
Axes of the slice: x: 4, y: 4, z: 16 (z_hi: 2, z_lo: 8; z = z_hi * 8 + z_lo), core: 2. Of those that a mesh axis runs over, the one named last changes fastest.
Arguments:
- layer_in: bfloat16 [8, 8192, 1024], P('section', 'expert'), may hold values from -6 to 6
- upstream: bfloat16 [8, 8192, 1024], P('section', 'expert'), may hold values from -0.796875 to 0.796875
- source_lengths: int32 [64], P('expert'), may hold values from 1 to 128
- target_lengths: int32 [64], P('expert'), may hold values from 1 to 128
- expert_ids: int32 [8, 8192, 2], P('section', 'expert'), may hold values from 0 to 15, all different within a row
- gate_values: float32 [8, 8192, 2], P('section', 'expert'), may hold values from 0.2 to 1
- expert_in: bfloat16 [8, 1024, 65536], P('section', None, 'expert'), may hold values from -0.1875 to 0.1875
- expert_out: bfloat16 [8, 65536, 1024], P('section', 'expert'), may hold values from -0.09375 to 0.09375
- attention_gain: float32 [8, 1024], P('section'), may hold values from 0.5 to 1.5
- mixture_gain: float32 [8, 1024], P('section'), may hold values from 0.5 to 1.5
- final_gain: float32 [1024], replicated, may hold values from 0.5 to 1.5
Outputs:
- gate_grad: float32 [8, 8192, 2], P('section', 'expert')
- input_grad: bfloat16 [8, 8192, 1024], P('section', 'expert')
Inputs may be any that keep to these rules, and one draw needn't show every extreme that they name: `expert_ids`: A token's two experts differ.
All inputs are finite; a program needn't handle non-finite values.
Results may differ from a plain program's by a relative error of at most 0.025.
The roundings to bfloat16 on the way count: a program that leaves them out, or rounds other values in their place, can miss the bound.
Values may be sent and summed in bfloat16 or wider, within the bound.
A program may use at most 64 MiB of HBM per device.

v0:
```python
import math

import jax
import jax.numpy as jnp
from jax import lax
from jax.sharding import PartitionSpec as P

HEAD_DIM = 128
HEADS = 8
GROUP = 4
SEQ = 128


EPSILON = 1e-06
HIGH = lax.Precision.HIGHEST


def broadcast(value, axis, source):
    kept = jnp.where(lax.axis_index(axis) == source, value, 0).astype(value.dtype)
    return lax.psum(kept, axis)


def rms_scale(values, scales):
    return values * lax.rsqrt(jnp.mean(values * values, axis=-1, keepdims=True) + EPSILON) * scales


def attend(inputs, states, scales, key_mask):
    sentences = key_mask.shape[0]
    queries = rms_scale(
        inputs.reshape(sentences, SEQ, HEADS, HEAD_DIM), scales.reshape(HEADS, HEAD_DIM)
    )
    memory = states.reshape(sentences, SEQ, HEADS, HEAD_DIM)
    scores = jnp.einsum("sihd,sjhd->shij", queries, memory, precision=HIGH) / math.sqrt(HEAD_DIM)
    weights = jnp.exp(scores) * key_mask[:, None, None, :]
    probability = weights / jnp.sum(weights, axis=-1, keepdims=True)
    rounded = lax.optimization_barrier(probability.astype(jnp.bfloat16)).astype(jnp.float32)
    mixed = jnp.einsum("shij,sjhd->sihd", rounded, memory, precision=HIGH)
    return inputs + mixed.reshape(inputs.shape)


def expert_tables(expert_ids, gate_values, expert_count, capacity):
    row_count = expert_ids.shape[0]
    experts = lax.broadcasted_iota(jnp.int32, (1, 1, expert_count), 2)
    chosen = (expert_ids[:, :, None] == experts).astype(jnp.int32)
    per_token = jnp.sum(chosen, axis=1)
    earlier = (
        lax.broadcasted_iota(jnp.int32, (row_count, row_count), 1)
        < lax.broadcasted_iota(jnp.int32, (row_count, row_count), 0)
    ).astype(jnp.int32)
    before = jnp.sum(earlier[:, :, None] * per_token[None, :, :], axis=1)
    slot_index = jnp.sum(chosen * before[:, None, :], axis=2)
    slot_iota = lax.broadcasted_iota(jnp.int32, (1, 1, 1, capacity), 3)
    matches = chosen[:, :, :, None] * (slot_index[:, :, None, None] == slot_iota).astype(jnp.int32)
    matches = matches.astype(jnp.float32).reshape(row_count, 2, expert_count * capacity)
    placing = jnp.sum(matches, axis=1)
    weighted = jnp.sum(matches * gate_values[:, :, None], axis=1)
    return (matches, placing, weighted)


def contract_last(left, right):
    return lax.dot_general(
        left, right, (((1,), (1,)), ((), ())), preferred_element_type=jnp.float32
    )


def body(
    layer_in,
    upstream,
    source_lengths,
    target_lengths,
    expert_ids,
    gate_values,
    expert_in,
    expert_out,
    attention_gain,
    mixture_gain,
    final_gain,
):
    section_count = lax.axis_size("section")
    expert_count = lax.axis_size("expert") // GROUP
    encoders = max(1, section_count // 4)
    section_index = lax.axis_index("section")
    is_decoder = section_index >= encoders
    is_bridge = section_index == encoders - 1
    is_last = section_index == section_count - 1
    inputs = layer_in[0]
    token_count = inputs.shape[0]
    width = inputs.shape[1]
    sentences = source_lengths.shape[0]
    capacity = 13 * token_count // (8 * expert_count)
    key_mask = (
        lax.broadcasted_iota(jnp.int32, (sentences, SEQ), 1) < source_lengths[:, None]
    ).astype(jnp.float32)
    loss_mask = (
        lax.broadcasted_iota(jnp.int32, (sentences, SEQ), 1) < target_lengths[:, None]
    ).astype(jnp.float32)
    loss_mask = loss_mask.reshape(token_count, 1)
    matches, placing, weighted = expert_tables(
        expert_ids[0], gate_values[0], expert_count, capacity
    )
    placing_low = placing.T.astype(jnp.bfloat16)
    first_layer = expert_in[0]
    second_layer = expert_out[0]
    attn_scales = attention_gain[0]
    mixture_scales = mixture_gain[0]

    def send_rows(slot_block):
        copies = jnp.repeat(slot_block, GROUP, axis=0)
        received = lax.all_to_all(copies, "expert", split_axis=0, concat_axis=0, tiled=True)
        arrived = received.reshape(-1, width)
        return arrived

    def return_rows(partials):
        received = lax.all_to_all(
            partials.reshape(-1, capacity, width), "expert", split_axis=0, concat_axis=0, tiled=True
        )
        blocks = received.reshape(expert_count, GROUP, capacity, width).astype(jnp.float32)
        return jnp.sum(blocks, axis=1).reshape(expert_count * capacity, width)

    inputs_wide = inputs.astype(jnp.float32)
    normed = rms_scale(inputs_wide, mixture_scales).astype(jnp.bfloat16)
    slot_block = jnp.dot(placing_low, normed, preferred_element_type=jnp.float32).astype(
        jnp.bfloat16
    )
    expert_rows = send_rows(slot_block.reshape(expert_count, capacity, width))
    hidden = jax.nn.relu(
        jnp.dot(expert_rows, first_layer, preferred_element_type=jnp.float32)
    ).astype(jnp.bfloat16)
    partials = jnp.dot(hidden, second_layer, preferred_element_type=jnp.float32).astype(
        jnp.bfloat16
    )
    summed = return_rows(partials)
    routed = jnp.dot(weighted, summed, precision=HIGH)
    moe_out = (inputs_wide + routed).astype(jnp.bfloat16)
    moe_wide = moe_out.astype(jnp.float32)
    own_states = rms_scale(moe_wide, final_gain).astype(jnp.bfloat16)
    states = broadcast(own_states, "section", encoders - 1)
    given = jnp.where(
        is_last, (upstream[0].astype(jnp.float32) * loss_mask).astype(jnp.bfloat16), upstream[0]
    )
    unused, pullback = jax.vjp(
        lambda values, memory: attend(values, memory, attn_scales, key_mask),
        moe_wide,
        states.astype(jnp.float32),
    )
    cross_grad, states_term = pullback(given.astype(jnp.float32))
    states_term = jnp.where(is_decoder, states_term, jnp.zeros_like(states_term))
    states_grad = lax.psum(states_term, "section")
    unused, pullback = jax.vjp(lambda values: rms_scale(values, final_gain), moe_wide)
    bridge_up = pullback(states_grad)[0].astype(jnp.bfloat16)
    moe_up = jnp.where(is_decoder, cross_grad.astype(jnp.bfloat16), given)
    moe_up = jnp.where(is_bridge, bridge_up, moe_up)
    up_wide = moe_up.astype(jnp.float32)
    selected = jnp.einsum("tke,ed->tkd", matches, summed, precision=HIGH)
    gate_grad = jnp.sum(up_wide[:, None, :] * selected, axis=2)
    slot_grads = jnp.dot(weighted.T, up_wide, precision=HIGH).astype(jnp.bfloat16)
    row_grads = send_rows(slot_grads.reshape(expert_count, capacity, width))
    hidden_grads = (contract_last(row_grads, second_layer) * (hidden > 0)).astype(jnp.bfloat16)
    partial_grads = contract_last(hidden_grads, first_layer).astype(jnp.bfloat16)
    summed_grads = return_rows(partial_grads)
    normed_grad = jnp.dot(placing, summed_grads, precision=HIGH)
    unused, pullback = jax.vjp(lambda values: rms_scale(values, mixture_scales), inputs_wide)
    input_grad = (up_wide + pullback(normed_grad)[0]).astype(jnp.bfloat16)
    return (gate_grad[None], input_grad[None])


def solution(mesh):
    in_specs = (
        P("section", "expert", None),
        P("section", "expert", None),
        P("expert"),
        P("expert"),
        P("section", "expert", None),
        P("section", "expert", None),
        P("section", None, "expert"),
        P("section", "expert", None),
        P("section", None),
        P("section", None),
        P(),
    )
    out_specs = (P("section", "expert", None), P("section", "expert", None))
    return jax.shard_map(body, mesh=mesh, in_specs=in_specs, out_specs=out_specs, check_vma=False)
```

profile of v0, /device:TPU:1, one launch (start us, length us, event | category | flops | bytes accessed | tf_op | source)
XLA Modules:
  0.0 798.1 jit_solution(7574086759273298406)
XLA Ops:
  7.2 0.8 fusion.77
  8.7 1.1 fusion.46
  9.8 2.2 multiply_reduce_fusion
  12.1 0.7 select_reduce_fusion
  12.8 1.4 multiply_reduce_fusion.6
  14.3 1.3 convolution_convert_fusion.1
  16.1 113.1 %all_to_all.20 = bf16[64,13,1024]{2,1,0:T(8,128)(2,1)} all-to-all(bf16[64,13,1024]{2,1,0:T(8,128)(2,1)S(1)} %bitcast.161), channel_id=1, replica_groups=mesh['section'=8,'expert'=64] {'expert'}, dimensions={0} | all-to-all | bytes 3407872 | tf_op jit(solution)/shard_map/all_to_all | solution.py:109
  129.2 3.7 reshape.297
  132.9 3.5 maximum_convert_fusion
  136.4 1.2 copy-done.25
  137.6 3.2 fusion.15
  140.8 3.6 reshape.298
  144.4 8.7 %all-to-all-start.1 = ((bf16[64,13,1024]{2,1,0:T(8,128)(2,1)}), bf16[64,13,1024]{2,1,0:T(8,128)(2,1)}, u32[]{:S(2)}, u32[]{:S(2)}) async-start(bf16[64,13,1024]{2,1,0:T(8,128)(2,1)} %reshape.298), calls=%async_computation.1 | async-start | bytes 4194304 | tf_op jit(solution)/shard_map/all_to_all | solution.py:114
  156.3 92.7 %all-to-all-done.1 = bf16[64,13,1024]{2,1,0:T(8,128)(2,1)} async-done(((bf16[64,13,1024]{2,1,0:T(8,128)(2,1)}), bf16[64,13,1024]{2,1,0:T(8,128)(2,1)}, u32[]{:S(2)}, u32[]{:S(2)}) %all-to-all-start.1) | async-done | bytes 1703968 | tf_op jit(solution)/shard_map/all_to_all | solution.py:114
  249.0 2.1 convert_reduce_fusion.1
  251.1 1.0 copy-done.1
  252.1 1.2 multiply_reduce_fusion.3
  253.4 0.8 copy_bitcast_fusion
  254.6 0.8 multiply_reduce_fusion.4
  255.4 1.0 copy.157
  256.4 1.5 copy.132
  257.9 1.0 copy.144
  259.0 0.7 fusion.78
  259.6 137.4 %all-reduce.3.cloned.1.call-done = bf16[128,8,128]{2,0,1:T(8,128)(2,1)} async-done(((bf16[128,8,128]{2,0,1:T(8,128)(2,1)}), bf16[128,8,128]{2,0,1:T(8,128)(2,1)}) %all-reduce.3.cloned.1.call-update) | async-done | bytes 262160 | tf_op jit(solution)/shard_map/psum | solution.py:20
  397.0 1.5 fusion.29
  398.5 1.8 multiply_reduce_fusion.5
  400.4 0.8 fusion.67
  401.2 0.7 fusion.42
  402.0 2.1 convolution_bitcast_fusion.4
  404.1 1.2 fusion.23
  405.3 2.0 copy.158
  407.4 1.9 multiply_reduce_fusion.1
  409.4 1.0 copy.159
  410.4 142.1 %all-reduce.5.cloned.1.call-done = f32[128,1024]{1,0:T(8,128)} async-done(((f32[128,1024]{1,0:T(8,128)}), f32[128,1024]{1,0:T(8,128)}) %all-reduce.5.cloned.1.call-update) | async-done | bytes 524304 | tf_op jit(solution)/shard_map/psum | solution.py:148
  552.5 1.2 multiply_reduce_fusion.2
  554.3 2.4 fusion.85
  556.7 1.3 convolution_convert_fusion
  558.0 1.2 reshape.305
  559.4 108.0 %all_to_all.21 = bf16[64,13,1024]{2,1,0:T(8,128)(2,1)} all-to-all(bf16[64,13,1024]{2,1,0:T(8,128)(2,1)S(1)} %bitcast.162), channel_id=1, replica_groups=mesh['section'=8,'expert'=64] {'expert'}, dimensions={0} | all-to-all | bytes 3407872 | tf_op jit(solution)/shard_map/all_to_all | solution.py:109
  667.4 3.7 reshape.307
  671.2 7.5 fusion.12
  678.7 3.6 reshape.308
  682.3 8.8 %all-to-all-start.3 = ((bf16[64,13,1024]{2,1,0:T(8,128)(2,1)}), bf16[64,13,1024]{2,1,0:T(8,128)(2,1)}, u32[]{:S(2)}, u32[]{:S(2)}) async-start(bf16[64,13,1024]{2,1,0:T(8,128)(2,1)} %reshape.308), calls=%async_computation.3 | async-start | bytes 4194304 | tf_op jit(solution)/shard_map/all_to_all | solution.py:114
  691.1 3.2 fusion.19
  694.2 92.7 %all-to-all-done.3 = bf16[64,13,1024]{2,1,0:T(8,128)(2,1)} async-done(((bf16[64,13,1024]{2,1,0:T(8,128)(2,1)}), bf16[64,13,1024]{2,1,0:T(8,128)(2,1)}, u32[]{:S(2)}, u32[]{:S(2)}) %all-to-all-start.3) | async-done | bytes 1703968 | tf_op jit(solution)/shard_map/all_to_all | solution.py:114
  786.9 2.1 convert_reduce_fusion
  789.1 1.2 fusion.49
  790.3 0.9 fusion.58
  (77 shorter events, 4.5 us)
Async XLA Ops:
  7.2 125.7 %copy-start = (bf16[1,1024,1024]{2,1,0:T(8,128)(2,1)S(1)}, bf16[1,1024,1024]{2,1,0:T(8,128)(2,1)}, u32[]{:S(2)}) copy-start(bf16[1,1024,1024]{2,1,0:T(8,128)(2,1)} %param.17) | copy-start | bytes 6291460
  9.8 6.3 copy-start.22
  9.8 6.3 copy-start.17
  132.9 4.7 copy-start.24
  136.4 1.2 copy-start.25
  144.4 10.1 %copy-start.9 = (f32[128,16,13]{0,1,2:T(8,128)S(1)}, f32[128,16,13]{0,1,2:T(8,128)}, u32[]{:S(2)}) copy-start(f32[128,16,13]{0,1,2:T(8,128)} %get-tuple-element.2) | copy-start | bytes 319492
  144.4 104.6 %all-to-all-start.1 = ((bf16[64,13,1024]{2,1,0:T(8,128)(2,1)}), bf16[64,13,1024]{2,1,0:T(8,128)(2,1)}, u32[]{:S(2)}, u32[]{:S(2)}) async-start(bf16[64,13,1024]{2,1,0:T(8,128)(2,1)} %reshape.298), calls=%async_computation.1 | async-start | bytes 4194304 | tf_op jit(solution)/shard_map/all_to_all | solution.py:114
  153.1 99.0 %copy-start.3 = (bf16[1,128,1024]{2,1,0:T(8,128)(2,1)S(1)}, bf16[1,128,1024]{2,1,0:T(8,128)(2,1)}, u32[]{:S(2)}) copy-start(bf16[1,128,1024]{2,1,0:T(8,128)(2,1)} %param.11) | copy-start | bytes 786436
  153.1 243.9 %all-reduce.3.cloned.1.call-start = ((), (), s32[]{:S(2)}) async-start(), calls=%async_computation.4 | async-start | bytes 524288 | tf_op jit(solution)/shard_map/psum | solution.py:20
  156.3 97.1 %copy-start.12 = (f32[1024]{0:T(1024)S(1)}, f32[1024]{0:T(1024)}, u32[]{:S(2)}) copy-start(f32[1024]{0:T(1024)} %param.21) | copy-start | bytes 12292
  251.1 1.0 copy-start.1
  253.3 1.1 copy-start.21
  253.3 1.1 copy-start.20
  254.2 298.2 %all-reduce.5.cloned.1.call-start = ((), (), s32[]{:S(2)}) async-start(), calls=%async_computation.5 | async-start | bytes 1048576 | tf_op jit(solution)/shard_map/psum | solution.py:148
  397.0 4.9 copy-start.7
  398.5 5.5 copy-start.11
  400.4 3.7 copy-start.13
  400.4 3.7 copy-start.8
  400.4 3.7 copy-start.19
  402.0 3.3 copy-start.16
  407.4 1.9 copy-start.14
  407.4 1.9 copy-start.6
  410.4 146.3 %copy-start.10 = (f32[128,208]{0,1:T(8,128)S(1)}, f32[128,208]{0,1:T(8,128)}, u32[]{:S(2)}) copy-start(f32[128,208]{0,1:T(8,128)} %reduce_sum.184) | copy-start | bytes 319492
  556.7 2.7 copy-start.4
  682.3 8.8 %copy-start.2 = (f32[16,13,1024]{2,1,0:T(8,128)S(1)}, f32[16,13,1024]{2,1,0:T(8,128)}, u32[]{:S(2)}) copy-start(f32[16,13,1024]{2,1,0:T(8,128)} %copy-done.1) | copy-start | bytes 2555908
  682.3 104.6 %all-to-all-start.3 = ((bf16[64,13,1024]{2,1,0:T(8,128)(2,1)}), bf16[64,13,1024]{2,1,0:T(8,128)(2,1)}, u32[]{:S(2)}, u32[]{:S(2)}) async-start(bf16[64,13,1024]{2,1,0:T(8,128)(2,1)} %reshape.308), calls=%async_computation.3 | async-start | bytes 4194304 | tf_op jit(solution)/shard_map/all_to_all | solution.py:114
  691.1 98.0 %copy-start.15 = (f32[1,1024]{1,0:T(1,128)S(1)}, f32[1,1024]{1,0:T(1,128)}, u32[]{:S(2)}) copy-start(f32[1,1024]{1,0:T(1,128)} %param.20) | copy-start | bytes 12292
  694.2 96.1 %copy-start.23 = (f32[128]{0:T(128)S(1)}, f32[128]{0:T(128)}, u32[]{:S(2)}) copy-start(f32[128]{0:T(128)} %copy-done.22) | copy-start | bytes 1540
  694.2 96.1 %copy-start.5 = (bf16[128,1024]{1,0:T(8,128)(2,1)S(1)}, bf16[128,1024]{1,0:T(8,128)(2,1)}, u32[]{:S(2)}) copy-start(bf16[128,1024]{1,0:T(8,128)(2,1)} %copy-done.4) | copy-start | bytes 786436
  694.2 96.1 %copy-start.18 = (f32[128]{0:T(128)S(1)}, f32[128]{0:T(128)}, u32[]{:S(2)}) copy-start(f32[128]{0:T(128)} %copy-done.17) | copy-start | bytes 1540
Sparse Core Ops, SparseCore 0:
  254.4 142.6 all-reduce.2
  407.5 144.9 all-reduce.4
where the time goes:
time: 799 us; the launch traced here: 798 us
  waiting for transfers between devices  465 us (58%)
  blocking collectives  221 us (28%)
  matrix products  30.9 us (4%)
  local copies, waits for them, and re-layouts  26.2 us (3%)
  other arithmetic  21.4 us (3%)
  starting transfers between devices  17.8 us (2%)
  between operations  15.8 us (2%)
    all_to_all x2, blocking collectives, send_rows(): lax.all_to_all(copies, 'expert', split_axis=0, concat_axis=0, tiled=True)  221 us
    all_to_all x2, waiting for transfers between devices, return_rows(): lax.all_to_all(partials.reshape(-1, capacity, width), 'expert', split_axi...  185 us
    psum x1, waiting for transfers between devices, body(): states_grad = lax.psum(states_term, 'section')  142 us
    psum x1, waiting for transfers between devices, broadcast(): return lax.psum(kept, axis)  137 us
    all_to_all x2, starting transfers between devices, return_rows(): lax.all_to_all(partials.reshape(-1, capacity, width), 'expert', split_axi...  17.5 us
  transfers between devices with their start and end apart: 4, of which 4 were waited for; matrix products, arithmetic and copies ran while one was open for 2% of the time, Pallas kernels for 0%

commit v1 on v0

v1 whole, which is shorter than its diff:
```python
import math

import jax
import jax.numpy as jnp
from jax import lax
from jax.experimental import pallas as pl
from jax.experimental.pallas import tpu as pltpu
from jax.sharding import PartitionSpec as P

MESH = pl.DeviceIdType.MESH
BF = jnp.bfloat16
F32 = jnp.float32
EPSILON = 1e-06
EXPERTS = 16
CAP = 13
PAD = 16
TOK = 128
D = 1024
HD = 128
ROWS = EXPERTS * PAD
BLOCK = ROWS
TILE = 256
SHIFTS = (2, 3, 1, 0)
NT = (((1,), (1,)), ((), ()))


def dot(a, b):
    return jnp.dot(a, b, preferred_element_type=F32)


def dot_nt(a, b):
    return lax.dot_general(a, b, NT, preferred_element_type=F32)


def split(v):
    high = v.astype(BF)
    return high, (v - high.astype(F32)).astype(BF)


def inverse_rms(v):
    return lax.rsqrt(jnp.mean(v * v, axis=-1, keepdims=True) + EPSILON)


def rms_back(v, g, cotangent):
    r = inverse_rms(v)
    scaled = g * cotangent
    return r * scaled - v * (r * r * r * jnp.mean(v * scaled, axis=-1, keepdims=True))


def remote(src, dst, send, recv, section, expert):
    return pltpu.make_async_remote_copy(
        src_ref=src,
        dst_ref=dst,
        send_sem=send,
        recv_sem=recv,
        device_id=(section, expert),
        device_id_type=MESH,
    )


def slot_tables(ids_ref, gates_ref):
    column = lax.broadcasted_iota(jnp.int32, (TOK, ROWS), 1)
    expert = column // PAD
    place = column - expert * PAD
    first = (ids_ref[:, 0:1] == expert).astype(F32)
    second = (ids_ref[:, 1:2] == expert).astype(F32)
    earlier = lax.broadcasted_iota(jnp.int32, (TOK, TOK), 1) < lax.broadcasted_iota(
        jnp.int32, (TOK, TOK), 0
    )
    before = dot(earlier.astype(F32).astype(BF), (first + second).astype(BF))
    kept = jnp.where(place < CAP, (before == place.astype(F32)).astype(F32), 0.0)
    first = first * kept
    second = second * kept
    weighted = first * gates_ref[:, 0:1] + second * gates_ref[:, 1:2]
    return first, second, weighted


class Exchange:
    scratch = [
        pltpu.VMEM((EXPERTS, PAD, D), BF),
        pltpu.VMEM((4, 2, 2, 4, PAD, D), BF),
        pltpu.VMEM((4, 2, 2, 4, PAD, D), BF),
        pltpu.VMEM((4, 2, 4, PAD, D), BF),
        pltpu.VMEM((4, 4, PAD, D), BF),
        pltpu.VMEM((4, 4, PAD, D), BF),
        pltpu.VMEM((4, 4, PAD, D), BF),
        pltpu.VMEM((EXPERTS, PAD, D), BF),
        pltpu.SemaphoreType.DMA((4, 4)),
        pltpu.SemaphoreType.DMA((4, 4)),
        pltpu.SemaphoreType.DMA((5, 4)),
        pltpu.SemaphoreType.DMA((5, 4)),
        pltpu.SemaphoreType.DMA((4, 4)),
        pltpu.SemaphoreType.DMA((4, 4)),
    ]

    def __init__(self, refs):
        (
            self.slots,
            self.rows,
            self.products,
            self.core_part,
            self.pair_out,
            self.pair_in,
            self.sums,
            self.back,
            self.a_send,
            self.a_recv,
            self.g_send,
            self.g_recv,
            self.f_send,
            self.f_recv,
        ) = refs
        self.section = lax.axis_index("section")
        p = lax.axis_index("expert")
        self.core = p % 2
        self.half = (p // 2) % 2
        self.ez = (p // 4) % 4
        self.ey = p // 16
        self.mine = self.ey * 4 + self.ez

    def device(self, ey, ez, half, core):
        return ((ey * 4 + ez) * 2 + half) * 2 + core

    def core_partner(self):
        return self.device(self.ey, self.ez, self.half, 1 - self.core)

    def pair_partner(self):
        return self.device(self.ey, self.ez, 1 - self.half, self.core)

    def greet(self):
        barrier = pltpu.get_barrier_semaphore()
        for dz in range(4):
            for dy in range(4):
                if dz or dy:
                    other = self.device(
                        (self.ey + dy) % 4, (self.ez + dz) % 4, self.half, self.core
                    )
                    pl.semaphore_signal(
                        barrier, inc=1, device_id=(self.section, other), device_id_type=MESH
                    )
        for other in (self.core_partner(), self.pair_partner()):
            pl.semaphore_signal(
                barrier, inc=1, device_id=(self.section, other), device_id_type=MESH
            )

    def meet(self):
        pl.semaphore_wait(pltpu.get_barrier_semaphore(), 17)

    def out_copy(self, t, dy):
        ey, ez = (self.ey + dy) % 4, (self.ez + SHIFTS[t]) % 4
        return remote(
            self.slots.at[ey * 4 + ez],
            self.rows.at[self.ez, self.core, self.half, self.ey],
            self.a_send.at[t, dy],
            self.a_recv.at[t, dy],
            self.section,
            self.device(ey, ez, self.half, self.core),
        )

    def source(self, t):
        return (self.ez + 4 - SHIFTS[t]) % 4

    def piece(self, t, kind):
        half = self.half if kind < 2 else 1 - self.half
        ref = self.rows.at[self.source(t), self.core, half]
        target = self.pair_partner() if kind == 0 else self.core_partner()
        return remote(
            ref, ref, self.g_send.at[kind, t], self.g_recv.at[kind, t], self.section, target
        )

    def core_copy(self, t):
        return remote(
            self.products.at[t, 1 - self.core],
            self.core_part.at[t],
            self.g_send.at[3, t],
            self.g_recv.at[3, t],
            self.section,
            self.core_partner(),
        )

    def pair_copy(self, t):
        return remote(
            self.pair_out.at[t],
            self.pair_in.at[t],
            self.g_send.at[4, t],
            self.g_recv.at[4, t],
            self.section,
            self.pair_partner(),
        )

    def back_copy(self, t, dy):
        ey = (self.ey + 4 - dy) % 4
        return remote(
            self.sums.at[t, ey],
            self.back.at[self.mine],
            self.f_send.at[t, dy],
            self.f_recv.at[t, dy],
            self.section,
            self.device(ey, self.source(t), self.half, self.core),
        )

    def far(self, t):
        return [dy for dy in range(4) if SHIFTS[t] or dy]

    def send_out(self):
        for t in range(4):
            for dy in self.far(t):
                self.out_copy(t, dy).start()
        self.rows[self.ez, self.core, self.half, self.ey] = self.slots[self.mine]

    def share(self, t):
        for dy in self.far(t):
            self.out_copy(t, dy).wait_recv()
        self.piece(t, 0).start()
        self.piece(t, 1).start()

    def pass_on(self, t):
        self.piece(t, 0).wait_recv()
        self.piece(t, 2).start()

    def multiply(self, t, experts):
        self.piece(t, 1).wait_recv()
        self.piece(t, 2).wait_recv()
        experts(t, self.source(t))
        self.core_copy(t).start()

    def core_sum(self, t):
        self.core_copy(t).wait_recv()
        other = 1 - self.half
        total = self.products[t, self.core, other].astype(F32) + self.core_part[t, other].astype(
            F32
        )
        self.pair_out[t] = total.astype(BF)
        self.pair_copy(t).start()

    def pair_sum(self, t):
        self.pair_copy(t).wait_recv()
        total = (
            self.products[t, self.core, self.half].astype(F32)
            + self.core_part[t, self.half].astype(F32)
            + self.pair_in[t].astype(F32)
        )
        self.sums[t] = total.astype(BF)
        for dy in self.far(t):
            self.back_copy(t, dy).start()
        if SHIFTS[t] == 0:
            self.back[self.mine] = self.sums[t, self.ey]

    def run(self, experts):
        for step in range(8):
            for stage, lag in (
                (self.share, 0),
                (self.pass_on, 1),
                (lambda t: self.multiply(t, experts), 2),
                (self.core_sum, 3),
                (self.pair_sum, 4),
            ):
                if 0 <= step - lag < 4:
                    stage(step - lag)
        for t in range(4):
            for dy in self.far(t):
                self.back_copy(t, dy).wait_recv()

    def finish(self):
        for t in range(4):
            for dy in self.far(t):
                self.out_copy(t, dy).wait_send()
                self.back_copy(t, dy).wait_send()
            for kind in range(3):
                self.piece(t, kind).wait_send()
            self.core_copy(t).wait_send()
            self.pair_copy(t).wait_send()


def forward_kernel(
    x_ref,
    ids_ref,
    gates_ref,
    mixture_ref,
    final_ref,
    w_in_hbm,
    w_out_hbm,
    moe_ref,
    states_ref,
    back_ref,
    hidden_hbm,
    w_in,
    w_out,
    hidden,
    w_sem,
    h_sem,
    *refs,
):
    ex = Exchange(refs)
    in_copy = pltpu.make_async_copy(w_in_hbm, w_in, w_sem.at[0])
    out_copy = pltpu.make_async_copy(w_out_hbm, w_out, w_sem.at[1])
    ex.greet()
    in_copy.start()
    out_copy.start()
    first, second, weighted = slot_tables(ids_ref, gates_ref)
    x = x_ref[...].astype(F32)
    normed = (x * inverse_rms(x) * mixture_ref[...]).astype(BF)
    placing_t = (first + second).T.astype(BF)
    ex.slots[...] = dot(placing_t, normed).astype(BF).reshape(EXPERTS, PAD, D)
    ex.meet()
    ex.send_out()
    in_copy.wait()
    out_copy.wait()

    def save(t, source):
        return pltpu.make_async_copy(hidden.at[source], hidden_hbm.at[source], h_sem.at[t])

    def experts(t, source):
        rows = ex.rows[source].reshape(BLOCK, D)

        def up(n, carry):
            tile = pl.ds(pl.multiple_of(n * TILE, TILE), TILE)
            hidden[source, :, tile] = jnp.maximum(dot(rows, w_in[:, tile]), 0.0).astype(BF)
            return carry

        lax.fori_loop(0, D // TILE, up, 0)
        units = hidden[source]

        def down(n, carry):
            tile = pl.ds(pl.multiple_of(n * TILE, TILE), TILE)
            part = dot(units, w_out[:, tile]).astype(BF)
            ex.products[t, :, :, :, :, tile] = part.reshape(2, 2, 4, PAD, TILE)
            return carry

        lax.fori_loop(0, D // TILE, down, 0)
        save(t, source).start()

    ex.run(experts)
    back_ref[...] = ex.back[...].reshape(ROWS, D)
    high, low = split(weighted)
    summed = back_ref[...]
    moe = (x + (dot(high, summed) + dot(low, summed))).astype(BF)
    moe_ref[...] = moe
    wide = moe.astype(F32)
    states = (wide * inverse_rms(wide) * final_ref[...]).astype(BF)
    for quarter in range(4):
        states_ref[quarter] = states[:, quarter * 256 : (quarter + 1) * 256]
    ex.finish()
    for t in range(4):
        save(t, ex.source(t)).wait()


def backward_kernel(
    x_ref,
    up_ref,
    ids_ref,
    gates_ref,
    mixture_ref,
    back_ref,
    w_in_hbm,
    w_out_hbm,
    hidden_hbm,
    gate_ref,
    grad_ref,
    w_in,
    w_out,
    hidden,
    units,
    w_sem,
    *refs,
):
    ex = Exchange(refs)
    in_copy = pltpu.make_async_copy(w_in_hbm, w_in, w_sem.at[0])
    out_copy = pltpu.make_async_copy(w_out_hbm, w_out, w_sem.at[1])
    hidden_copy = pltpu.make_async_copy(hidden_hbm, hidden, w_sem.at[2])
    ex.greet()
    in_copy.start()
    out_copy.start()
    hidden_copy.start()
    first, second, weighted = slot_tables(ids_ref, gates_ref)
    up_low = up_ref[...]
    up = up_low.astype(F32)
    high, low = split(weighted.T)
    grads = dot(high, up_low) + dot(low, up_low)
    ex.slots[...] = grads.astype(BF).reshape(EXPERTS, PAD, D)
    ex.meet()
    ex.send_out()
    summed = back_ref[...]
    gate_ref[:, 0:1] = jnp.sum(up * dot(first.astype(BF), summed), axis=1, keepdims=True)
    gate_ref[:, 1:2] = jnp.sum(up * dot(second.astype(BF), summed), axis=1, keepdims=True)
    in_copy.wait()
    out_copy.wait()
    hidden_copy.wait()

    def experts(t, source):
        rows = ex.rows[source].reshape(BLOCK, D)

        def down(n, carry):
            tile = pl.ds(pl.multiple_of(n * TILE, TILE), TILE)
            part = dot_nt(rows, w_out[tile, :])
            alive = hidden[source, :, tile].astype(F32) > 0.0
            units[:, tile] = jnp.where(alive, part, 0.0).astype(BF)
            return carry

        lax.fori_loop(0, D // TILE, down, 0)
        held = units[...]

        def across(n, carry):
            tile = pl.ds(pl.multiple_of(n * TILE, TILE), TILE)
            part = dot_nt(held, w_in[tile, :]).astype(BF)
            ex.products[t, :, :, :, :, tile] = part.reshape(2, 2, 4, PAD, TILE)
            return carry

        lax.fori_loop(0, D // TILE, across, 0)

    ex.run(experts)
    placing = (first + second).astype(BF)
    normed_grad = dot(placing, ex.back[...].reshape(ROWS, D))
    x = x_ref[...].astype(F32)
    grad_ref[...] = (up + rms_back(x, mixture_ref[...], normed_grad)).astype(BF)
    ex.finish()


def cross_kernel(
    source_len,
    target_len,
    states_ref,
    moe_ref,
    up_in_ref,
    attention_ref,
    final_ref,
    up_ref,
    held,
    terms,
    terms_in,
    cross_out,
    cross_in,
    final_out,
    final_in,
    total,
    s_send,
    s_recv,
    t_send,
    t_recv,
    x_sem,
    f_send,
    f_recv,
):
    s = lax.axis_index("section")
    p = lax.axis_index("expert")
    x = s % 4
    low_z = s < 4
    high_z = s >= 4
    bridge = s == 1
    decoder = s >= 2
    low_decoder = jnp.logical_and(low_z, decoder)
    relay = jnp.logical_and(low_z, s != 1)

    barrier = pltpu.get_barrier_semaphore()
    for d in range(1, 8):
        pl.semaphore_signal(barrier, inc=1, device_id=((s + d) % 8, p), device_id_type=MESH)
    pl.semaphore_wait(barrier, 7)

    first_sends = [(0, 0), (2, 2), (3, 3), (1, 5)]
    later_sends = [(0, 2), (1, 2), (3, 2), (0, 3), (1, 3), (2, 3)]
    sends = first_sends + later_sends

    def bridge_copy(i):
        quarter, target = sends[i]
        return remote(
            states_ref.at[quarter], held.at[quarter], s_send.at[i], s_recv.at[quarter], target, p
        )

    def onward(slot, target):
        return remote(held.at[x], held.at[x], s_send.at[slot], s_recv.at[x], target, p)

    def arrived(quarter):
        onto = held.at[quarter]
        return remote(onto, onto, s_send.at[0], s_recv.at[quarter], s, p)

    @pl.when(bridge)
    def _():
        for i in range(len(sends)):
            bridge_copy(i).start()

    @pl.when(relay)
    def _():
        arrived(x).wait_recv()
        onward(0, x + 4).start()

    @pl.when(high_z)
    def _():
        arrived(x).wait_recv()
        for d in range(1, 4):
            onward(d, 4 + (x + d) % 4).start()

    def term_high(k):
        return remote(
            terms.at[k], terms_in.at[k - 1], t_send.at[k], t_recv.at[k - 1], 4 + (x + k) % 4, p
        )

    def term_low(k):
        return remote(
            terms.at[k], terms_in.at[s - 2], t_send.at[k], t_recv.at[s - 2], (x + k) % 4, p
        )

    def term_in(slot):
        return remote(terms.at[0], terms_in.at[slot], t_send.at[0], t_recv.at[slot], s, p)

    @pl.when(decoder)
    def _():
        tokens = lax.broadcasted_iota(jnp.int32, (TOK, 1), 0)
        keys = lax.broadcasted_iota(jnp.int32, (1, TOK), 1)
        key_mask = (keys < source_len[0]).astype(F32)
        loss_mask = jnp.logical_or(tokens < target_len[0], s < 7).astype(F32)
        for k in range(4):
            j = (x + k) % 4
            if k:
                arrived(j).wait_recv()
            for h in range(2):
                lanes = pl.ds(pl.multiple_of(j * 256 + h * HD, HD), HD)
                a = moe_ref[:, lanes].astype(F32)
                m = held[j, :, h * HD : (h + 1) * HD]
                g = attention_ref[:, lanes]
                given = (up_in_ref[:, lanes].astype(F32) * loss_mask).astype(BF)
                q = a * inverse_rms(a) * g
                q_high, q_low = split(q)
                scores = (dot_nt(q_high, m) + dot_nt(q_low, m)) * (1.0 / math.sqrt(HD))
                weights = jnp.exp(scores) * key_mask
                probs = weights / jnp.sum(weights, axis=-1, keepdims=True)
                rounded = probs.astype(BF)
                d_probs = dot_nt(given, m).astype(BF).astype(F32)
                inner = jnp.sum(d_probs * probs, axis=-1, keepdims=True)
                d_scores = probs * (d_probs - inner) * (1.0 / math.sqrt(HD))
                s_high, s_low = split(d_scores)
                d_q = dot(s_high, m) + dot(s_low, m)
                t_high, t_low = split(d_scores.T)
                rounded_t = rounded.astype(F32).T.astype(BF)
                d_m = (
                    dot(rounded_t, given)
                    + dot(t_high, q_high)
                    + dot(t_high, q_low)
                    + dot(t_low, q_high)
                )
                up_ref[:, lanes] = (given.astype(F32) + rms_back(a, g, d_q)).astype(BF)
                if k == 0:
                    total[:, h * HD : (h + 1) * HD] = d_m
                else:
                    terms[k, :, h * HD : (h + 1) * HD] = d_m.astype(BF)
            if k:

                @pl.when(high_z)
                def _():
                    term_high(k).start()

                @pl.when(low_z)
                def _():
                    term_low(k).start()

    def cross_copy(target):
        return remote(cross_out, cross_in, x_sem.at[0], x_sem.at[1], target, p)

    def final_copy():
        return remote(final_out, final_in.at[x], f_send, f_recv.at[x], 1, p)

    def final_arrived(quarter):
        return remote(final_out, final_in.at[quarter], f_send, f_recv.at[quarter], s, p)

    @pl.when(high_z)
    def _():
        for slot in range(3):
            term_in(slot).wait_recv()
        summed = total[...]
        for slot in range(3):
            summed = summed + terms_in[slot].astype(F32)
        cross_out[...] = summed.astype(BF)
        cross_copy(x).start()
        cross_copy(x).wait_send()

    @pl.when(s < 2)
    def _():
        total[...] = jnp.zeros_like(total)

    @pl.when(low_z)
    def _():
        for slot in range(2):

            @pl.when(s != slot + 2)
            def _():
                term_in(slot).wait_recv()
                total[...] += terms_in[slot].astype(F32)

        cross_copy(s).wait_recv()
        total[...] += cross_in[...].astype(F32)

    @pl.when(relay)
    def _():
        final_out[...] = total[...].astype(BF)
        final_copy().start()
        final_copy().wait_send()

    @pl.when(s == 0)
    def _():
        up_ref[...] = up_in_ref[...]

    @pl.when(bridge)
    def _():
        pieces = []
        for quarter in range(4):
            if quarter == 1:
                pieces.append(total[...])
            else:
                final_arrived(quarter).wait_recv()
                pieces.append(final_in[quarter].astype(F32))
        cotangent = jnp.concatenate(pieces, axis=1)
        v = moe_ref[...].astype(F32)
        up_ref[...] = rms_back(v, final_ref[...], cotangent).astype(BF)
        for i in range(len(sends)):
            bridge_copy(i).wait_send()

    @pl.when(relay)
    def _():
        onward(0, x + 4).wait_send()

    @pl.when(high_z)
    def _():
        for d in range(1, 4):
            onward(d, 4 + (x + d) % 4).wait_send()
            term_high(d).wait_send()

    @pl.when(low_decoder)
    def _():
        for d in range(1, 4):
            term_low(d).wait_send()


VM = pl.BlockSpec(memory_space=pltpu.VMEM)
SM = pl.BlockSpec(memory_space=pltpu.SMEM)
HB = pl.BlockSpec(memory_space=pl.ANY)


def shape(dims, dtype):
    return jax.ShapeDtypeStruct(dims, dtype)


def params(number):
    return pltpu.CompilerParams(
        collective_id=number, has_side_effects=True, vmem_limit_bytes=44 * 1024 * 1024
    )


def body(
    layer_in,
    upstream,
    source_lengths,
    target_lengths,
    expert_ids,
    gate_values,
    expert_in,
    expert_out,
    attention_gain,
    mixture_gain,
    final_gain,
):
    x = layer_in[0]
    ids = expert_ids[0]
    gates = gate_values[0]
    final = final_gain.reshape(1, D)
    flops = 4 * 1024 * 1024 * 1024
    moe, states, back, hidden = pl.pallas_call(
        forward_kernel,
        out_shape=(
            shape((TOK, D), BF),
            shape((4, TOK, 256), BF),
            shape((ROWS, D), BF),
            shape((4, BLOCK, D), BF),
        ),
        in_specs=[VM] * 5 + [HB] * 2,
        out_specs=(VM, VM, VM, HB),
        scratch_shapes=[
            pltpu.VMEM((D, D), BF),
            pltpu.VMEM((D, D), BF),
            pltpu.VMEM((4, BLOCK, D), BF),
            pltpu.SemaphoreType.DMA((2,)),
            pltpu.SemaphoreType.DMA((4,)),
        ]
        + Exchange.scratch,
        compiler_params=params(0),
        cost_estimate=pl.CostEstimate(flops=flops, bytes_accessed=8 << 20, transcendentals=0),
        name="moe_forward",
    )(x, ids, gates, mixture_gain, final, expert_in[0], expert_out[0])
    moe_up = pl.pallas_call(
        cross_kernel,
        out_shape=shape((TOK, D), BF),
        in_specs=[SM, SM] + [VM] * 5,
        out_specs=VM,
        scratch_shapes=[
            pltpu.VMEM((4, TOK, 256), BF),
            pltpu.VMEM((4, TOK, 256), BF),
            pltpu.VMEM((3, TOK, 256), BF),
            pltpu.VMEM((TOK, 256), BF),
            pltpu.VMEM((TOK, 256), BF),
            pltpu.VMEM((TOK, 256), BF),
            pltpu.VMEM((4, TOK, 256), BF),
            pltpu.VMEM((TOK, 256), F32),
            pltpu.SemaphoreType.DMA((10,)),
            pltpu.SemaphoreType.DMA((4,)),
            pltpu.SemaphoreType.DMA((4,)),
            pltpu.SemaphoreType.DMA((3,)),
            pltpu.SemaphoreType.DMA((2,)),
            pltpu.SemaphoreType.DMA,
            pltpu.SemaphoreType.DMA((4,)),
        ],
        compiler_params=params(1),
        cost_estimate=pl.CostEstimate(flops=1 << 28, bytes_accessed=2 << 20, transcendentals=0),
        name="cross_attention",
    )(source_lengths, target_lengths, states, moe, upstream[0], attention_gain, final)
    gate_grad, input_grad = pl.pallas_call(
        backward_kernel,
        out_shape=(shape((TOK, 2), F32), shape((TOK, D), BF)),
        in_specs=[VM] * 6 + [HB] * 3,
        out_specs=(VM, VM),
        scratch_shapes=[
            pltpu.VMEM((D, D), BF),
            pltpu.VMEM((D, D), BF),
            pltpu.VMEM((4, BLOCK, D), BF),
            pltpu.VMEM((BLOCK, D), BF),
            pltpu.SemaphoreType.DMA((3,)),
        ]
        + Exchange.scratch,
        compiler_params=params(2),
        cost_estimate=pl.CostEstimate(flops=flops, bytes_accessed=8 << 20, transcendentals=0),
        name="moe_backward",
    )(x, moe_up, ids, gates, mixture_gain, back, expert_in[0], expert_out[0], hidden)
    return (gate_grad[None], input_grad[None])


def solution(mesh):
    in_specs = (
        P("section", "expert", None),
        P("section", "expert", None),
        P("expert"),
        P("expert"),
        P("section", "expert", None),
        P("section", "expert", None),
        P("section", None, "expert"),
        P("section", "expert", None),
        P("section", None),
        P("section", None),
        P(),
    )
    out_specs = (P("section", "expert", None), P("section", "expert", None))
    return jax.shard_map(body, mesh=mesh, in_specs=in_specs, out_specs=out_specs, check_vma=False)
```

time: 799 us -> 213 us (0.27)
  the two profiles are of different devices: /device:TPU:1 before, /device:TPU:66 now
where the time goes in v1:
time: 213 us; the launch traced here: 212 us
  Pallas kernels  202 us (95%)
  local copies, waits for them, and re-layouts  8.42 us (4%)
    pallas_call x1, Pallas kernels, body(): pl.pallas_call(forward_kernel, out_shape=(shape((TOK, D), BF), shape((4,...  82.2 us
    pallas_call x1, Pallas kernels, body(): pl.pallas_call(backward_kernel, out_shape=(shape((TOK, 2), F32), shape((T...  73.8 us
    pallas_call x1, Pallas kernels, body(): pl.pallas_call(cross_kernel, out_shape=shape((TOK, D), BF), in_specs=[SM,...  45.9 us
    unnamed x22, local copies, waits for them, and re-layouts  8.42 us

profile of v1, /device:TPU:66, one launch (start us, length us, event | category | flops | bytes accessed | tf_op | source)
XLA Modules:
  0.0 212.3 jit_solution(8585232744452891564)
XLA Ops:
  1.9 0.8 copy.13
  2.7 0.8 copy.14
  3.5 0.0 copy-start.1
  3.5 0.7 copy-done.1
  4.2 0.0 copy-start.3
  4.2 1.6 copy-done.3
  5.8 0.0 copy-start.5
  5.8 1.6 copy-done.5
  7.4 0.0 copy-start.7
  7.4 0.9 copy-done.7
  8.3 0.0 copy-start.8
  8.3 0.7 copy-done.8
  9.0 0.0 copy-start
  9.0 0.0 copy-start.2
  9.0 0.0 copy-start.4
  9.0 0.0 copy-start.6
  9.0 82.2 %moe_forward.1 = (bf16[128,1024]{1,0:T(8,128)(2,1)S(1)}, bf16[4,128,256]{2,1,0:T(8,128)(2,1)S(1)}, bf16[256,1024]{1,0:T(8,128)(2,1)S(1)}, bf16[4,256,1024]{2,1,0:T(8,128)(2,1)S(1)}) custom-call(bf16[128,1024]{1,0:T(8,128)(2,1)S(1)} %bitcast.22, s32[128,2]{1,0:T(8,128)S(1)} %bitcast.11, f32[128,2]{1,0:T(8,128)S(1)} %bitcast.13, f32[1,1024]{1,0:T(1,128)S(1)} %copy-done.8, ...), custom_call_target="tpu_custom_call" | custom-call | flops 4294967296 | bytes 8388608 | tf_op jit(solution)/shard_map/moe_forward/pallas_call | solution.py:665
  91.3 0.0 copy-done
  91.3 0.0 copy-done.2
  91.3 45.9 %cross_attention.1.up_ref = bf16[128,1024]{1,0:T(8,128)(2,1)S(1)} custom-call(s32[1]{0:T(128)S(6)} %copy.17.source_len, s32[1]{0:T(128)S(6)} %copy.18.target_len, bf16[4,128,256]{2,1,0:T(8,128)(2,1)S(1)} %get-tuple-element.8.states_ref, bf16[128,1024]{1,0:T(8,128)(2,1)S(1)} %get-tuple-element.9.moe_ref, bf16[128,1024]{1,0:T(8,128)(2,1)S(1)} %bitcast.9, ...), custom_call_target="tpu_custom_call" | custom-call | flops 268435456 | bytes 2097152 | tf_op jit(solution)/shard_map/cross_attention/pallas_call | solution.py:687
  137.2 0.0 copy-done.4
  137.2 0.0 copy-done.6
  137.2 73.8 %moe_backward.1 = (f32[128,2]{1,0:T(8,128)S(1)}, bf16[128,1024]{1,0:T(8,128)(2,1)S(1)}) custom-call(bf16[128,1024]{1,0:T(8,128)(2,1)S(1)} %bitcast.23, bf16[128,1024]{1,0:T(8,128)(2,1)S(1)} %cross_attention.1.up_ref, s32[128,2]{1,0:T(8,128)S(1)} %bitcast.12, f32[128,2]{1,0:T(8,128)S(1)} %bitcast.14, f32[1,1024]{1,0:T(1,128)S(1)} %copy-done.8, ...), custom_call_target="tpu_custom_call" | custom-call | flops 4294967296 | bytes 8388608 | tf_op jit(solution)/shard_map/moe_backward/pallas_call | solution.py:713
  211.0 0.6 copy.15
  211.6 0.7 copy.19
Async XLA Ops:
  3.5 0.7 copy-start.1
  4.2 1.6 copy-start.3
  5.8 1.6 copy-start.5
  7.4 0.9 copy-start.7
  8.3 0.7 copy-start.8
  9.0 82.3 %copy-start = (bf16[1,128,1024]{2,1,0:T(8,128)(2,1)S(1)}, bf16[1,128,1024]{2,1,0:T(8,128)(2,1)}, u32[]{:S(2)}) copy-start(bf16[1,128,1024]{2,1,0:T(8,128)(2,1)} %param.12) | copy-start | bytes 786436
  9.0 82.3 %copy-start.2 = (f32[1,1024]{1,0:T(1,128)S(1)}, f32[1,1024]{1,0:T(1,128)}, u32[]{:S(2)}) copy-start(f32[1,1024]{1,0:T(1,128)} %attention_ref.1) | copy-start | bytes 12292
  9.0 128.2 %copy-start.4 = (bf16[1,1024,1024]{2,1,0:T(8,128)(2,1)S(1)}, bf16[1,1024,1024]{2,1,0:T(8,128)(2,1)}, u32[]{:S(2)}) copy-start(bf16[1,1024,1024]{2,1,0:T(8,128)(2,1)} %param.17) | copy-start | bytes 6291460
  9.0 128.2 %copy-start.6 = (bf16[1,1024,1024]{2,1,0:T(8,128)(2,1)S(1)}, bf16[1,1024,1024]{2,1,0:T(8,128)(2,1)}, u32[]{:S(2)}) copy-start(bf16[1,1024,1024]{2,1,0:T(8,128)(2,1)} %param.18) | copy-start | bytes 6291460

commit v2 on v1

--- a/solution.py
+++ b/solution.py
@@ -17,6 +17,7 @@
 TOK = 128
 D = 1024
 HD = 128
+PACKED = 896
 ROWS = EXPERTS * PAD
 BLOCK = ROWS
 TILE = 256
@@ -75,21 +76,72 @@
     return first, second, weighted
 
 
+def pack_matrix():
+    row = lax.broadcasted_iota(jnp.int32, (PACKED, 128), 0)
+    column = lax.broadcasted_iota(jnp.int32, (PACKED, 128), 1)
+    return pack_rule(row, column)
+
+
+def unpack_matrix():
+    row = lax.broadcasted_iota(jnp.int32, (128, PACKED), 0)
+    column = lax.broadcasted_iota(jnp.int32, (128, PACKED), 1)
+    return pack_rule(column, row)
+
+
+def pack_rule(spare, plain):
+    chunk = spare // 128
+    inside = spare - chunk * 128
+    block = inside // PAD
+    place = inside - block * PAD
+    slot = plain - block * PAD
+    wanted = chunk + 7 * (place - CAP)
+    hit = jnp.where(place == CAP, 1.0, jnp.where(place == CAP + 1, 1.0, 0.0))
+    hit = jnp.where(wanted == slot, hit, 0.0)
+    return jnp.where(wanted < CAP, hit, 0.0).astype(BF)
+
+
+def pack(values, matrix):
+    spare = (lax.broadcasted_iota(jnp.int32, (128, 128), 0) % PAD) >= CAP
+    halves = []
+    for half in range(2):
+        part = values[half * 128 : (half + 1) * 128]
+        moved = dot(matrix, part[:, PACKED:])
+        chunks = [
+            jnp.where(
+                spare,
+                moved[k * 128 : (k + 1) * 128],
+                part[:, k * 128 : (k + 1) * 128].astype(F32),
+            ).astype(BF)
+            for k in range(7)
+        ]
+        halves.append(jnp.concatenate(chunks, axis=1))
+    return jnp.concatenate(halves, axis=0)
+
+
+def unpack_last(packed, matrix):
+    halves = []
+    for half in range(2):
+        part = packed[half * 128 : (half + 1) * 128]
+        stacked = jnp.concatenate([part[:, k * 128 : (k + 1) * 128] for k in range(7)], axis=0)
+        halves.append(dot(matrix, stacked).astype(BF))
+    return jnp.concatenate(halves, axis=0)
+
+
 class Exchange:
     scratch = [
-        pltpu.VMEM((EXPERTS, PAD, D), BF),
-        pltpu.VMEM((4, 2, 2, 4, PAD, D), BF),
-        pltpu.VMEM((4, 2, 2, 4, PAD, D), BF),
-        pltpu.VMEM((4, 2, 4, PAD, D), BF),
-        pltpu.VMEM((4, 4, PAD, D), BF),
-        pltpu.VMEM((4, 4, PAD, D), BF),
-        pltpu.VMEM((4, 4, PAD, D), BF),
-        pltpu.VMEM((EXPERTS, PAD, D), BF),
+        pltpu.VMEM((EXPERTS, PAD, PACKED), BF),
+        pltpu.VMEM((4, 2, 2, 4, PAD, PACKED), BF),
+        pltpu.VMEM((4, 2, 2, 4, PAD, PACKED), BF),
+        pltpu.VMEM((4, 2, 4, PAD, PACKED), BF),
+        pltpu.VMEM((4, 2, 4, PAD, PACKED), BF),
+        pltpu.VMEM((4, 2, 4, PAD, PACKED), BF),
+        pltpu.VMEM((4, 2, 4, PAD, PACKED), BF),
+        pltpu.VMEM((EXPERTS, PAD, PACKED), BF),
+        pltpu.SemaphoreType.DMA((4, 4)),
+        pltpu.SemaphoreType.DMA((4, 2, 4)),
         pltpu.SemaphoreType.DMA((4, 4)),
         pltpu.SemaphoreType.DMA((4, 4)),
-        pltpu.SemaphoreType.DMA((5, 4)),
-        pltpu.SemaphoreType.DMA((5, 4)),
-        pltpu.SemaphoreType.DMA((4, 4)),
+        pltpu.SemaphoreType.DMA((4, 2, 4)),
         pltpu.SemaphoreType.DMA((4, 4)),
     ]
 
@@ -129,78 +181,105 @@
 
     def greet(self):
         barrier = pltpu.get_barrier_semaphore()
-        for dz in range(4):
-            for dy in range(4):
-                if dz or dy:
-                    other = self.device(
-                        (self.ey + dy) % 4, (self.ez + dz) % 4, self.half, self.core
-                    )
-                    pl.semaphore_signal(
-                        barrier, inc=1, device_id=(self.section, other), device_id_type=MESH
-                    )
-        for other in (self.core_partner(), self.pair_partner()):
+
+        def signal(other):
             pl.semaphore_signal(
                 barrier, inc=1, device_id=(self.section, other), device_id_type=MESH
             )
 
+        for dz in range(4):
+            for dy in range(4):
+                for dh in range(2):
+                    if dz or dy or dh:
+                        signal(
+                            self.device(
+                                (self.ey + dy) % 4,
+                                (self.ez + dz) % 4,
+                                (self.half + dh) % 2,
+                                self.core,
+                            )
+                        )
+        signal(self.core_partner())
+
     def meet(self):
-        pl.semaphore_wait(pltpu.get_barrier_semaphore(), 17)
+        pl.semaphore_wait(pltpu.get_barrier_semaphore(), 32)
+
+    def source(self, t):
+        return (self.ez + 4 - SHIFTS[t]) % 4
+
+    def near(self, t):
+        return 1 - (self.ez + 4 - SHIFTS[t]) // 4
+
+    def far(self, t):
+        return [dy for dy in range(4) if SHIFTS[t] or dy]
+
+    def copy(self, src, dst, send, recv, target):
+        return remote(src, dst, send, recv, self.section, target)
 
     def out_copy(self, t, dy):
         ey, ez = (self.ey + dy) % 4, (self.ez + SHIFTS[t]) % 4
-        return remote(
+        half = (self.ez + SHIFTS[t]) // 4 if SHIFTS[t] else self.half
+        return self.copy(
             self.slots.at[ey * 4 + ez],
             self.rows.at[self.ez, self.core, self.half, self.ey],
             self.a_send.at[t, dy],
-            self.a_recv.at[t, dy],
-            self.section,
-            self.device(ey, ez, self.half, self.core),
-        )
-
-    def source(self, t):
-        return (self.ez + 4 - SHIFTS[t]) % 4
-
-    def piece(self, t, kind):
-        half = self.half if kind < 2 else 1 - self.half
-        ref = self.rows.at[self.source(t), self.core, half]
-        target = self.pair_partner() if kind == 0 else self.core_partner()
-        return remote(
-            ref, ref, self.g_send.at[kind, t], self.g_recv.at[kind, t], self.section, target
+            self.a_recv.at[t, self.half, dy],
+            self.device(ey, ez, half, self.core),
+        )
+
+    def out_arrival(self, t, half, dy):
+        block = self.rows.at[self.source(t), self.core, half, (self.ey + 4 - dy) % 4]
+        return self.copy(
+            block, block, self.a_send.at[t, dy], self.a_recv.at[t, half, dy], self.core_partner()
+        )
+
+    def pair_share(self, t, half=None):
+        block = self.rows.at[self.source(t), self.core]
+        if half is not None:
+            block = block.at[half]
+        return self.copy(
+            block, block, self.g_send.at[0, t], self.g_recv.at[0, t], self.pair_partner()
+        )
+
+    def core_share(self, t):
+        block = self.rows.at[self.source(t), self.core]
+        return self.copy(
+            block, block, self.g_send.at[1, t], self.g_recv.at[1, t], self.core_partner()
         )
 
     def core_copy(self, t):
-        return remote(
+        return self.copy(
             self.products.at[t, 1 - self.core],
             self.core_part.at[t],
-            self.g_send.at[3, t],
-            self.g_recv.at[3, t],
-            self.section,
+            self.g_send.at[2, t],
+            self.g_recv.at[2, t],
             self.core_partner(),
         )
 
-    def pair_copy(self, t):
-        return remote(
-            self.pair_out.at[t],
-            self.pair_in.at[t],
-            self.g_send.at[4, t],
-            self.g_recv.at[4, t],
-            self.section,
-            self.pair_partner(),
-        )
-
-    def back_copy(self, t, dy):
+    def pair_copy(self, t, half=None):
+        src, dst = self.pair_out.at[t], self.pair_in.at[t]
+        if half is not None:
+            src, dst = src.at[half], dst.at[half]
+        return self.copy(
+            src, dst, self.g_send.at[3, t], self.g_recv.at[3, t], self.pair_partner()
+        )
+
+    def back_copy(self, t, half, dy):
         ey = (self.ey + 4 - dy) % 4
-        return remote(
-            self.sums.at[t, ey],
+        return self.copy(
+            self.sums.at[t, half, ey],
             self.back.at[self.mine],
-            self.f_send.at[t, dy],
+            self.f_send.at[t, half, dy],
             self.f_recv.at[t, dy],
-            self.section,
-            self.device(ey, self.source(t), self.half, self.core),
-        )
-
-    def far(self, t):
-        return [dy for dy in range(4) if SHIFTS[t] or dy]
+            self.device(ey, self.source(t), half, self.core),
+        )
+
+    def back_arrival(self, t, dy):
+        ey, ez = (self.ey + dy) % 4, (self.ez + SHIFTS[t]) % 4
+        block = self.back.at[ey * 4 + ez]
+        return self.copy(
+            block, block, self.f_send.at[t, 0, dy], self.f_recv.at[t, dy], self.core_partner()
+        )
 
     def send_out(self):
         for t in range(4):
@@ -209,42 +288,78 @@
         self.rows[self.ez, self.core, self.half, self.ey] = self.slots[self.mine]
 
     def share(self, t):
-        for dy in self.far(t):
-            self.out_copy(t, dy).wait_recv()
-        self.piece(t, 0).start()
-        self.piece(t, 1).start()
+        if SHIFTS[t] == 0:
+            for dy in self.far(t):
+                self.out_arrival(t, self.half, dy).wait_recv()
+            self.pair_share(t, self.half).start()
+            return
+
+        @pl.when(self.half == self.near(t))
+        def _():
+            for half in range(2):
+                for dy in self.far(t):
+                    self.out_arrival(t, half, dy).wait_recv()
+            self.pair_share(t).start()
+            self.core_share(t).start()
 
     def pass_on(self, t):
-        self.piece(t, 0).wait_recv()
-        self.piece(t, 2).start()
+        if SHIFTS[t] == 0:
+            self.pair_share(t, 1 - self.half).wait_recv()
+            self.core_share(t).start()
+            return
+
+        @pl.when(self.half != self.near(t))
+        def _():
+            self.pair_share(t).wait_recv()
+            self.core_share(t).start()
 
     def multiply(self, t, experts):
-        self.piece(t, 1).wait_recv()
-        self.piece(t, 2).wait_recv()
+        self.core_share(t).wait_recv()
         experts(t, self.source(t))
         self.core_copy(t).start()
 
     def core_sum(self, t):
         self.core_copy(t).wait_recv()
-        other = 1 - self.half
-        total = self.products[t, self.core, other].astype(F32) + self.core_part[t, other].astype(
-            F32
-        )
-        self.pair_out[t] = total.astype(BF)
-        self.pair_copy(t).start()
+        if SHIFTS[t] == 0:
+            other = 1 - self.half
+            self.pair_out[t, other] = (
+                self.products[t, self.core, other].astype(F32)
+                + self.core_part[t, other].astype(F32)
+            ).astype(BF)
+            self.pair_copy(t, other).start()
+            return
+
+        @pl.when(self.half != self.near(t))
+        def _():
+            self.pair_out[t] = (
+                self.products[t, self.core].astype(F32) + self.core_part[t].astype(F32)
+            ).astype(BF)
+            self.pair_copy(t).start()
 
     def pair_sum(self, t):
-        self.pair_copy(t).wait_recv()
-        total = (
-            self.products[t, self.core, self.half].astype(F32)
-            + self.core_part[t, self.half].astype(F32)
-            + self.pair_in[t].astype(F32)
-        )
-        self.sums[t] = total.astype(BF)
-        for dy in self.far(t):
-            self.back_copy(t, dy).start()
         if SHIFTS[t] == 0:
-            self.back[self.mine] = self.sums[t, self.ey]
+            self.pair_copy(t, self.half).wait_recv()
+            self.sums[t, self.half] = (
+                self.products[t, self.core, self.half].astype(F32)
+                + self.core_part[t, self.half].astype(F32)
+                + self.pair_in[t, self.half].astype(F32)
+            ).astype(BF)
+            for dy in self.far(t):
+                self.back_copy(t, self.half, dy).start()
+            self.back[self.mine] = self.sums[t, self.half, self.ey]
+            return
+
+        @pl.when(self.half == self.near(t))
+        def _():
+            self.pair_copy(t).wait_recv()
+            self.sums[t] = (
+                self.products[t, self.core].astype(F32)
+                + self.core_part[t].astype(F32)
+                + self.pair_in[t].astype(F32)
+            ).astype(BF)
+            for half in range(2):
+                for dy in self.far(t):
+                    self.back_copy(t, half, dy).start()
 
     def run(self, experts):
         for step in range(8):
@@ -259,17 +374,40 @@
                     stage(step - lag)
         for t in range(4):
             for dy in self.far(t):
-                self.back_copy(t, dy).wait_recv()
+                self.back_arrival(t, dy).wait_recv()
 
     def finish(self):
         for t in range(4):
             for dy in self.far(t):
                 self.out_copy(t, dy).wait_send()
-                self.back_copy(t, dy).wait_send()
-            for kind in range(3):
-                self.piece(t, kind).wait_send()
+            self.core_share(t).wait_send()
             self.core_copy(t).wait_send()
-            self.pair_copy(t).wait_send()
+            if SHIFTS[t] == 0:
+                self.pair_share(t, self.half).wait_send()
+                self.pair_copy(t, 1 - self.half).wait_send()
+                for dy in self.far(t):
+                    self.back_copy(t, self.half, dy).wait_send()
+                continue
+
+            @pl.when(self.half == self.near(t))
+            def _():
+                self.pair_share(t).wait_send()
+                for half in range(2):
+                    for dy in self.far(t):
+                        self.back_copy(t, half, dy).wait_send()
+
+            @pl.when(self.half != self.near(t))
+            def _():
+                self.pair_copy(t).wait_send()
+
+    def received(self, t, full, matrix):
+        packed = self.rows[self.source(t)].reshape(BLOCK, PACKED)
+        full[:, :PACKED] = packed
+        full[:, PACKED:] = unpack_last(packed, matrix)
+
+    def returned(self, matrix):
+        packed = self.back[...].reshape(ROWS, PACKED)
+        return jnp.concatenate([packed, unpack_last(packed, matrix)], axis=1)
 
 
 def forward_kernel(
@@ -287,6 +425,10 @@
     w_in,
     w_out,
     hidden,
+    full,
+    product,
+    packing,
+    unpacking,
     w_sem,
     h_sem,
     *refs,
@@ -301,9 +443,12 @@
     x = x_ref[...].astype(F32)
     normed = (x * inverse_rms(x) * mixture_ref[...]).astype(BF)
     placing_t = (first + second).T.astype(BF)
-    ex.slots[...] = dot(placing_t, normed).astype(BF).reshape(EXPERTS, PAD, D)
+    packing[...] = pack_matrix()
+    slots = pack(dot(placing_t, normed).astype(BF), packing[...])
+    ex.slots[...] = slots.reshape(EXPERTS, PAD, PACKED)
     ex.meet()
     ex.send_out()
+    unpacking[...] = unpack_matrix()
     in_copy.wait()
     out_copy.wait()
 
@@ -311,7 +456,8 @@
         return pltpu.make_async_copy(hidden.at[source], hidden_hbm.at[source], h_sem.at[t])
 
     def experts(t, source):
-        rows = ex.rows[source].reshape(BLOCK, D)
+        ex.received(t, full, unpacking[...])
+        rows = full[...]
 
         def up(n, carry):
             tile = pl.ds(pl.multiple_of(n * TILE, TILE), TILE)
@@ -323,17 +469,17 @@
 
         def down(n, carry):
             tile = pl.ds(pl.multiple_of(n * TILE, TILE), TILE)
-            part = dot(units, w_out[:, tile]).astype(BF)
-            ex.products[t, :, :, :, :, tile] = part.reshape(2, 2, 4, PAD, TILE)
+            product[:, tile] = dot(units, w_out[:, tile]).astype(BF)
             return carry
 
         lax.fori_loop(0, D // TILE, down, 0)
+        ex.products[t] = pack(product[...], packing[...]).reshape(2, 2, 4, PAD, PACKED)
         save(t, source).start()
 
     ex.run(experts)
-    back_ref[...] = ex.back[...].reshape(ROWS, D)
+    summed = ex.returned(unpacking[...])
+    back_ref[...] = summed
     high, low = split(weighted)
-    summed = back_ref[...]
     moe = (x + (dot(high, summed) + dot(low, summed))).astype(BF)
     moe_ref[...] = moe
     wide = moe.astype(F32)
@@ -361,6 +507,10 @@
     w_out,
     hidden,
     units,
+    full,
+    product,
+    packing,
+    unpacking,
     w_sem,
     *refs,
 ):
@@ -377,9 +527,11 @@
     up = up_low.astype(F32)
     high, low = split(weighted.T)
     grads = dot(high, up_low) + dot(low, up_low)
-    ex.slots[...] = grads.astype(BF).reshape(EXPERTS, PAD, D)
+    packing[...] = pack_matrix()
+    ex.slots[...] = pack(grads.astype(BF), packing[...]).reshape(EXPERTS, PAD, PACKED)
     ex.meet()
     ex.send_out()
+    unpacking[...] = unpack_matrix()
     summed = back_ref[...]
     gate_ref[:, 0:1] = jnp.sum(up * dot(first.astype(BF), summed), axis=1, keepdims=True)
     gate_ref[:, 1:2] = jnp.sum(up * dot(second.astype(BF), summed), axis=1, keepdims=True)
@@ -388,7 +540,8 @@
     hidden_copy.wait()
 
     def experts(t, source):
-        rows = ex.rows[source].reshape(BLOCK, D)
+        ex.received(t, full, unpacking[...])
+        rows = full[...]
 
         def down(n, carry):
             tile = pl.ds(pl.multiple_of(n * TILE, TILE), TILE)
@@ -402,15 +555,15 @@
 
         def across(n, carry):
             tile = pl.ds(pl.multiple_of(n * TILE, TILE), TILE)
-            part = dot_nt(held, w_in[tile, :]).astype(BF)
-            ex.products[t, :, :, :, :, tile] = part.reshape(2, 2, 4, PAD, TILE)
+            product[:, tile] = dot_nt(held, w_in[tile, :]).astype(BF)
             return carry
 
         lax.fori_loop(0, D // TILE, across, 0)
+        ex.products[t] = pack(product[...], packing[...]).reshape(2, 2, 4, PAD, PACKED)
 
     ex.run(experts)
     placing = (first + second).astype(BF)
-    normed_grad = dot(placing, ex.back[...].reshape(ROWS, D))
+    normed_grad = dot(placing, ex.returned(unpacking[...]))
     x = x_ref[...].astype(F32)
     grad_ref[...] = (up + rms_back(x, mixture_ref[...], normed_grad)).astype(BF)
     ex.finish()
@@ -640,7 +793,7 @@
 
 def params(number):
     return pltpu.CompilerParams(
-        collective_id=number, has_side_effects=True, vmem_limit_bytes=44 * 1024 * 1024
+        collective_id=number, has_side_effects=True, vmem_limit_bytes=60 * 1024 * 1024
     )
 
 
@@ -676,6 +829,10 @@
             pltpu.VMEM((D, D), BF),
             pltpu.VMEM((D, D), BF),
             pltpu.VMEM((4, BLOCK, D), BF),
+            pltpu.VMEM((BLOCK, D), BF),
+            pltpu.VMEM((BLOCK, D), BF),
+            pltpu.VMEM((PACKED, 128), BF),
+            pltpu.VMEM((128, PACKED), BF),
             pltpu.SemaphoreType.DMA((2,)),
             pltpu.SemaphoreType.DMA((4,)),
         ]
@@ -720,6 +877,10 @@
             pltpu.VMEM((D, D), BF),
             pltpu.VMEM((4, BLOCK, D), BF),
             pltpu.VMEM((BLOCK, D), BF),
+            pltpu.VMEM((BLOCK, D), BF),
+            pltpu.VMEM((BLOCK, D), BF),
+            pltpu.VMEM((PACKED, 128), BF),
+            pltpu.VMEM((128, PACKED), BF),
             pltpu.SemaphoreType.DMA((3,)),
         ]
         + Exchange.scratch,

time: 213 us -> 209 us (0.981)
  the two profiles are of different devices: /device:TPU:66 before, /device:TPU:32 now
where the time goes in v2:
time: 209 us
  Pallas kernels  201 us (96%)
  local copies, waits for them, and re-layouts  5.97 us (3%)
    pallas_call x1, Pallas kernels, body(): pl.pallas_call(forward_kernel, out_shape=(shape((TOK, D), BF), shape((4,...  82 us
    pallas_call x1, Pallas kernels, body(): pl.pallas_call(backward_kernel, out_shape=(shape((TOK, 2), F32), shape((T...  73.6 us
    pallas_call x1, Pallas kernels, body(): pl.pallas_call(cross_kernel, out_shape=shape((TOK, D), BF), in_specs=[SM,...  45 us
    unnamed x4, local copies, waits for them, and re-layouts  5.97 us

profile of v2, /device:TPU:32, one launch (start us, length us, event | category | flops | bytes accessed | tf_op | source)
XLA Modules:
  0.0 208.5 jit_solution(3284442663857374781)
XLA Ops:
  1.9 1.4 copy.13
  3.3 1.4 copy.14
  4.7 82.0 %moe_forward.1 = (bf16[128,1024]{1,0:T(8,128)(2,1)}, bf16[4,128,256]{2,1,0:T(8,128)(2,1)}, bf16[256,1024]{1,0:T(8,128)(2,1)}, bf16[4,256,1024]{2,1,0:T(8,128)(2,1)}) custom-call(bf16[128,1024]{1,0:T(8,128)(2,1)} %bitcast.22, s32[128,2]{1,0:T(8,128)} %bitcast.11, f32[128,2]{1,0:T(8,128)} %bitcast.13, f32[1,1024]{1,0:T(1,128)} %mixture_ref.3, ...), custom_call_target="tpu_custom_call" | custom-call | flops 4294967296 | bytes 8388608 | tf_op jit(solution)/shard_map/moe_forward/pallas_call | solution.py:818
  86.8 45.0 %cross_attention.1.up_ref = bf16[128,1024]{1,0:T(8,128)(2,1)} custom-call(s32[1]{0:T(128)S(6)} %copy.17.source_len, s32[1]{0:T(128)S(6)} %copy.18.target_len, bf16[4,128,256]{2,1,0:T(8,128)(2,1)} %get-tuple-element.8.states_ref, bf16[128,1024]{1,0:T(8,128)(2,1)} %get-tuple-element.9.moe_ref, bf16[128,1024]{1,0:T(8,128)(2,1)} %bitcast.9, ...), custom_call_target="tpu_custom_call" | custom-call | flops 268435456 | bytes 2097152 | tf_op jit(solution)/shard_map/cross_attention/pallas_call | solution.py:844
  131.8 73.6 %moe_backward.1 = (f32[128,2]{1,0:T(8,128)}, bf16[128,1024]{1,0:T(8,128)(2,1)}) custom-call(bf16[128,1024]{1,0:T(8,128)(2,1)} %bitcast.23, bf16[128,1024]{1,0:T(8,128)(2,1)} %cross_attention.1.up_ref, s32[128,2]{1,0:T(8,128)} %bitcast.12, f32[128,2]{1,0:T(8,128)} %bitcast.14, f32[1,1024]{1,0:T(1,128)} %mixture_ref.3, ...), custom_call_target="tpu_custom_call" | custom-call | flops 4294967296 | bytes 8388608 | tf_op jit(solution)/shard_map/moe_backward/pallas_call | solution.py:870
  205.4 1.5 copy.15
  206.9 1.7 copy.19

commit v3 on v2

--- a/solution.py
+++ b/solution.py
@@ -59,12 +59,17 @@
     )
 
 
+def spread(row):
+    column = jnp.broadcast_to(row, (TOK, TOK)).T
+    return jnp.concatenate([column, column], axis=1)
+
+
 def slot_tables(ids_ref, gates_ref):
     column = lax.broadcasted_iota(jnp.int32, (TOK, ROWS), 1)
     expert = column // PAD
     place = column - expert * PAD
-    first = (ids_ref[:, 0:1] == expert).astype(F32)
-    second = (ids_ref[:, 1:2] == expert).astype(F32)
+    first = (spread(ids_ref[0:1, :].astype(F32)) == expert.astype(F32)).astype(F32)
+    second = (spread(ids_ref[1:2, :].astype(F32)) == expert.astype(F32)).astype(F32)
     earlier = lax.broadcasted_iota(jnp.int32, (TOK, TOK), 1) < lax.broadcasted_iota(
         jnp.int32, (TOK, TOK), 0
     )
@@ -72,7 +77,7 @@
     kept = jnp.where(place < CAP, (before == place.astype(F32)).astype(F32), 0.0)
     first = first * kept
     second = second * kept
-    weighted = first * gates_ref[:, 0:1] + second * gates_ref[:, 1:2]
+    weighted = first * spread(gates_ref[0:1, :]) + second * spread(gates_ref[1:2, :])
     return first, second, weighted
 
 
@@ -201,9 +206,6 @@
                         )
         signal(self.core_partner())
 
-    def meet(self):
-        pl.semaphore_wait(pltpu.get_barrier_semaphore(), 32)
-
     def source(self, t):
         return (self.ez + 4 - SHIFTS[t]) % 4
 
@@ -410,166 +412,26 @@
         return jnp.concatenate([packed, unpack_last(packed, matrix)], axis=1)
 
 
-def forward_kernel(
-    x_ref,
-    ids_ref,
-    gates_ref,
-    mixture_ref,
-    final_ref,
-    w_in_hbm,
-    w_out_hbm,
-    moe_ref,
-    states_ref,
-    back_ref,
-    hidden_hbm,
-    w_in,
-    w_out,
-    hidden,
-    full,
-    product,
-    packing,
-    unpacking,
-    w_sem,
-    h_sem,
-    *refs,
-):
-    ex = Exchange(refs)
-    in_copy = pltpu.make_async_copy(w_in_hbm, w_in, w_sem.at[0])
-    out_copy = pltpu.make_async_copy(w_out_hbm, w_out, w_sem.at[1])
-    ex.greet()
-    in_copy.start()
-    out_copy.start()
-    first, second, weighted = slot_tables(ids_ref, gates_ref)
-    x = x_ref[...].astype(F32)
-    normed = (x * inverse_rms(x) * mixture_ref[...]).astype(BF)
-    placing_t = (first + second).T.astype(BF)
-    packing[...] = pack_matrix()
-    slots = pack(dot(placing_t, normed).astype(BF), packing[...])
-    ex.slots[...] = slots.reshape(EXPERTS, PAD, PACKED)
-    ex.meet()
-    ex.send_out()
-    unpacking[...] = unpack_matrix()
-    in_copy.wait()
-    out_copy.wait()
-
-    def save(t, source):
-        return pltpu.make_async_copy(hidden.at[source], hidden_hbm.at[source], h_sem.at[t])
-
-    def experts(t, source):
-        ex.received(t, full, unpacking[...])
-        rows = full[...]
-
-        def up(n, carry):
-            tile = pl.ds(pl.multiple_of(n * TILE, TILE), TILE)
-            hidden[source, :, tile] = jnp.maximum(dot(rows, w_in[:, tile]), 0.0).astype(BF)
-            return carry
-
-        lax.fori_loop(0, D // TILE, up, 0)
-        units = hidden[source]
-
-        def down(n, carry):
-            tile = pl.ds(pl.multiple_of(n * TILE, TILE), TILE)
-            product[:, tile] = dot(units, w_out[:, tile]).astype(BF)
-            return carry
-
-        lax.fori_loop(0, D // TILE, down, 0)
-        ex.products[t] = pack(product[...], packing[...]).reshape(2, 2, 4, PAD, PACKED)
-        save(t, source).start()
-
-    ex.run(experts)
-    summed = ex.returned(unpacking[...])
-    back_ref[...] = summed
-    high, low = split(weighted)
-    moe = (x + (dot(high, summed) + dot(low, summed))).astype(BF)
-    moe_ref[...] = moe
-    wide = moe.astype(F32)
-    states = (wide * inverse_rms(wide) * final_ref[...]).astype(BF)
-    for quarter in range(4):
-        states_ref[quarter] = states[:, quarter * 256 : (quarter + 1) * 256]
-    ex.finish()
-    for t in range(4):
-        save(t, ex.source(t)).wait()
-
-
-def backward_kernel(
-    x_ref,
-    up_ref,
-    ids_ref,
-    gates_ref,
-    mixture_ref,
-    back_ref,
-    w_in_hbm,
-    w_out_hbm,
-    hidden_hbm,
-    gate_ref,
-    grad_ref,
-    w_in,
-    w_out,
-    hidden,
-    units,
-    full,
-    product,
-    packing,
-    unpacking,
-    w_sem,
-    *refs,
-):
-    ex = Exchange(refs)
-    in_copy = pltpu.make_async_copy(w_in_hbm, w_in, w_sem.at[0])
-    out_copy = pltpu.make_async_copy(w_out_hbm, w_out, w_sem.at[1])
-    hidden_copy = pltpu.make_async_copy(hidden_hbm, hidden, w_sem.at[2])
-    ex.greet()
-    in_copy.start()
-    out_copy.start()
-    hidden_copy.start()
-    first, second, weighted = slot_tables(ids_ref, gates_ref)
-    up_low = up_ref[...]
-    up = up_low.astype(F32)
-    high, low = split(weighted.T)
-    grads = dot(high, up_low) + dot(low, up_low)
-    packing[...] = pack_matrix()
-    ex.slots[...] = pack(grads.astype(BF), packing[...]).reshape(EXPERTS, PAD, PACKED)
-    ex.meet()
-    ex.send_out()
-    unpacking[...] = unpack_matrix()
-    summed = back_ref[...]
-    gate_ref[:, 0:1] = jnp.sum(up * dot(first.astype(BF), summed), axis=1, keepdims=True)
-    gate_ref[:, 1:2] = jnp.sum(up * dot(second.astype(BF), summed), axis=1, keepdims=True)
-    in_copy.wait()
-    out_copy.wait()
-    hidden_copy.wait()
-
-    def experts(t, source):
-        ex.received(t, full, unpacking[...])
-        rows = full[...]
-
-        def down(n, carry):
-            tile = pl.ds(pl.multiple_of(n * TILE, TILE), TILE)
-            part = dot_nt(rows, w_out[tile, :])
-            alive = hidden[source, :, tile].astype(F32) > 0.0
-            units[:, tile] = jnp.where(alive, part, 0.0).astype(BF)
-            return carry
-
-        lax.fori_loop(0, D // TILE, down, 0)
-        held = units[...]
-
-        def across(n, carry):
-            tile = pl.ds(pl.multiple_of(n * TILE, TILE), TILE)
-            product[:, tile] = dot_nt(held, w_in[tile, :]).astype(BF)
-            return carry
-
-        lax.fori_loop(0, D // TILE, across, 0)
-        ex.products[t] = pack(product[...], packing[...]).reshape(2, 2, 4, PAD, PACKED)
-
-    ex.run(experts)
-    placing = (first + second).astype(BF)
-    normed_grad = dot(placing, ex.returned(unpacking[...]))
-    x = x_ref[...].astype(F32)
-    grad_ref[...] = (up + rms_back(x, mixture_ref[...], normed_grad)).astype(BF)
-    ex.finish()
-
-
-def cross_kernel(
+CROSS_SCRATCH = [
+    pltpu.VMEM((4, TOK, 256), BF),
+    pltpu.VMEM((4, TOK, 256), BF),
+    pltpu.VMEM((3, TOK, 256), BF),
+    pltpu.VMEM((TOK, 256), BF),
+    pltpu.VMEM((TOK, 256), BF),
+    pltpu.VMEM((TOK, 256), BF),
+    pltpu.VMEM((4, TOK, 256), BF),
+    pltpu.VMEM((TOK, 256), F32),
+    pltpu.SemaphoreType.DMA((10,)),
+    pltpu.SemaphoreType.DMA((4,)),
+    pltpu.SemaphoreType.DMA((4,)),
+    pltpu.SemaphoreType.DMA((3,)),
+    pltpu.SemaphoreType.DMA((2,)),
+    pltpu.SemaphoreType.DMA,
+    pltpu.SemaphoreType.DMA((4,)),
+]
+
+
+def cross_part(
     source_len,
     target_len,
     states_ref,
@@ -603,11 +465,6 @@
     decoder = s >= 2
     low_decoder = jnp.logical_and(low_z, decoder)
     relay = jnp.logical_and(low_z, s != 1)
-
-    barrier = pltpu.get_barrier_semaphore()
-    for d in range(1, 8):
-        pl.semaphore_signal(barrier, inc=1, device_id=((s + d) % 8, p), device_id_type=MESH)
-    pl.semaphore_wait(barrier, 7)
 
     first_sends = [(0, 0), (2, 2), (3, 3), (1, 5)]
     later_sends = [(0, 2), (1, 2), (3, 2), (0, 3), (1, 3), (2, 3)]
@@ -782,6 +639,156 @@
             term_low(d).wait_send()
 
 
+def whole_kernel(
+    source_len,
+    target_len,
+    x_ref,
+    up_in_ref,
+    ids_ref,
+    gates_ref,
+    attention_ref,
+    mixture_ref,
+    final_ref,
+    w_in_hbm,
+    w_out_hbm,
+    gate_ref,
+    grad_ref,
+    w_in,
+    w_out,
+    hidden,
+    units,
+    full,
+    product,
+    packing,
+    unpacking,
+    matches,
+    weights,
+    moe_ref,
+    states_ref,
+    summed_ref,
+    up_ref,
+    w_sem,
+    *refs,
+):
+    cross_refs = refs[: len(CROSS_SCRATCH)]
+    refs = refs[len(CROSS_SCRATCH) :]
+    ahead = Exchange(refs[: len(refs) // 2])
+    behind = Exchange(refs[len(refs) // 2 :])
+    in_copy = pltpu.make_async_copy(w_in_hbm, w_in, w_sem.at[0])
+    out_copy = pltpu.make_async_copy(w_out_hbm, w_out, w_sem.at[1])
+    barrier = pltpu.get_barrier_semaphore()
+    s = lax.axis_index("section")
+    p = lax.axis_index("expert")
+    ahead.greet()
+    for d in range(1, 8):
+        pl.semaphore_signal(barrier, inc=1, device_id=((s + d) % 8, p), device_id_type=MESH)
+    in_copy.start()
+    out_copy.start()
+
+    first, second, weighted = slot_tables(ids_ref, gates_ref)
+    x = x_ref[...].astype(F32)
+    normed = (x * inverse_rms(x) * mixture_ref[...]).astype(BF)
+    placing_t = (first + second).T.astype(BF)
+    packing[...] = pack_matrix()
+    slots = pack(dot(placing_t, normed).astype(BF), packing[...])
+    ahead.slots[...] = slots.reshape(EXPERTS, PAD, PACKED)
+    pl.semaphore_wait(barrier, 39)
+    ahead.send_out()
+    matches[0] = first.astype(BF)
+    matches[1] = second.astype(BF)
+    weights[...] = weighted
+    unpacking[...] = unpack_matrix()
+    in_copy.wait()
+    out_copy.wait()
+
+    def experts(t, source):
+        ahead.received(t, full, unpacking[...])
+        rows = full[...]
+
+        def up(n, carry):
+            tile = pl.ds(pl.multiple_of(n * TILE, TILE), TILE)
+            hidden[source, :, tile] = jnp.maximum(dot(rows, w_in[:, tile]), 0.0).astype(BF)
+            return carry
+
+        lax.fori_loop(0, D // TILE, up, 0)
+        held = hidden[source]
+
+        def down(n, carry):
+            tile = pl.ds(pl.multiple_of(n * TILE, TILE), TILE)
+            product[:, tile] = dot(held, w_out[:, tile]).astype(BF)
+            return carry
+
+        lax.fori_loop(0, D // TILE, down, 0)
+        ahead.products[t] = pack(product[...], packing[...]).reshape(2, 2, 4, PAD, PACKED)
+
+    ahead.run(experts)
+    summed = ahead.returned(unpacking[...])
+    summed_ref[...] = summed
+    high, low = split(weights[...])
+    moe = (x_ref[...].astype(F32) + (dot(high, summed) + dot(low, summed))).astype(BF)
+    moe_ref[...] = moe
+
+    @pl.when(s == 1)
+    def _():
+        wide = moe_ref[...].astype(F32)
+        states = (wide * inverse_rms(wide) * final_ref[...]).astype(BF)
+        for quarter in range(4):
+            states_ref[quarter] = states[:, quarter * 256 : (quarter + 1) * 256]
+
+    cross_part(
+        source_len,
+        target_len,
+        states_ref,
+        moe_ref,
+        up_in_ref,
+        attention_ref,
+        final_ref,
+        up_ref,
+        *cross_refs,
+    )
+
+    up_low = up_ref[...]
+    high, low = split(weights[...].T)
+    grads = dot(high, up_low) + dot(low, up_low)
+    behind.slots[...] = pack(grads.astype(BF), packing[...]).reshape(EXPERTS, PAD, PACKED)
+    behind.send_out()
+    wide_up = up_low.astype(F32)
+    for choice in range(2):
+        chosen = dot(matches[choice], summed_ref[...])
+        column = jnp.sum(wide_up * chosen, axis=1, keepdims=True)
+        gate_ref[choice : choice + 1, :] = jnp.broadcast_to(column, (TOK, TOK)).T[0:1, :]
+
+    def experts_back(t, source):
+        behind.received(t, full, unpacking[...])
+        rows = full[...]
+
+        def down(n, carry):
+            tile = pl.ds(pl.multiple_of(n * TILE, TILE), TILE)
+            part = dot_nt(rows, w_out[tile, :])
+            alive = hidden[source, :, tile].astype(F32) > 0.0
+            units[:, tile] = jnp.where(alive, part, 0.0).astype(BF)
+            return carry
+
+        lax.fori_loop(0, D // TILE, down, 0)
+        held = units[...]
+
+        def across(n, carry):
+            tile = pl.ds(pl.multiple_of(n * TILE, TILE), TILE)
+            product[:, tile] = dot_nt(held, w_in[tile, :]).astype(BF)
+            return carry
+
+        lax.fori_loop(0, D // TILE, across, 0)
+        behind.products[t] = pack(product[...], packing[...]).reshape(2, 2, 4, PAD, PACKED)
+
+    behind.run(experts_back)
+    placing = (matches[0].astype(F32) + matches[1].astype(F32)).astype(BF)
+    normed_grad = dot(placing, behind.returned(unpacking[...]))
+    back = rms_back(x_ref[...].astype(F32), mixture_ref[...], normed_grad)
+    grad_ref[...] = (up_ref[...].astype(F32) + back).astype(BF)
+    ahead.finish()
+    behind.finish()
+
+
 VM = pl.BlockSpec(memory_space=pltpu.VMEM)
 SM = pl.BlockSpec(memory_space=pltpu.SMEM)
 HB = pl.BlockSpec(memory_space=pl.ANY)
@@ -810,85 +817,51 @@
     mixture_gain,
     final_gain,
 ):
-    x = layer_in[0]
-    ids = expert_ids[0]
-    gates = gate_values[0]
-    final = final_gain.reshape(1, D)
-    flops = 4 * 1024 * 1024 * 1024
-    moe, states, back, hidden = pl.pallas_call(
-        forward_kernel,
-        out_shape=(
-            shape((TOK, D), BF),
-            shape((4, TOK, 256), BF),
-            shape((ROWS, D), BF),
-            shape((4, BLOCK, D), BF),
-        ),
-        in_specs=[VM] * 5 + [HB] * 2,
-        out_specs=(VM, VM, VM, HB),
+    vmem = pltpu.VMEM
+    gate_grad, input_grad = pl.pallas_call(
+        whole_kernel,
+        out_shape=(shape((2, TOK), F32), shape((TOK, D), BF)),
+        in_specs=[SM] * 2 + [VM] * 7 + [HB] * 2,
+        out_specs=(VM, VM),
         scratch_shapes=[
-            pltpu.VMEM((D, D), BF),
-            pltpu.VMEM((D, D), BF),
-            pltpu.VMEM((4, BLOCK, D), BF),
-            pltpu.VMEM((BLOCK, D), BF),
-            pltpu.VMEM((BLOCK, D), BF),
-            pltpu.VMEM((PACKED, 128), BF),
-            pltpu.VMEM((128, PACKED), BF),
+            vmem((D, D), BF),
+            vmem((D, D), BF),
+            vmem((4, BLOCK, D), BF),
+            vmem((BLOCK, D), BF),
+            vmem((BLOCK, D), BF),
+            vmem((BLOCK, D), BF),
+            vmem((PACKED, 128), BF),
+            vmem((128, PACKED), BF),
+            vmem((2, TOK, ROWS), BF),
+            vmem((TOK, ROWS), F32),
+            vmem((TOK, D), BF),
+            vmem((4, TOK, 256), BF),
+            vmem((ROWS, D), BF),
+            vmem((TOK, D), BF),
             pltpu.SemaphoreType.DMA((2,)),
-            pltpu.SemaphoreType.DMA((4,)),
         ]
+        + CROSS_SCRATCH
+        + Exchange.scratch
         + Exchange.scratch,
         compiler_params=params(0),
-        cost_estimate=pl.CostEstimate(flops=flops, bytes_accessed=8 << 20, transcendentals=0),
-        name="moe_forward",
-    )(x, ids, gates, mixture_gain, final, expert_in[0], expert_out[0])
-    moe_up = pl.pallas_call(
-        cross_kernel,
-        out_shape=shape((TOK, D), BF),
-        in_specs=[SM, SM] + [VM] * 5,
-        out_specs=VM,
-        scratch_shapes=[
-            pltpu.VMEM((4, TOK, 256), BF),
-            pltpu.VMEM((4, TOK, 256), BF),
-            pltpu.VMEM((3, TOK, 256), BF),
-            pltpu.VMEM((TOK, 256), BF),
-            pltpu.VMEM((TOK, 256), BF),
-            pltpu.VMEM((TOK, 256), BF),
-            pltpu.VMEM((4, TOK, 256), BF),
-            pltpu.VMEM((TOK, 256), F32),
-            pltpu.SemaphoreType.DMA((10,)),
-            pltpu.SemaphoreType.DMA((4,)),
-            pltpu.SemaphoreType.DMA((4,)),
-            pltpu.SemaphoreType.DMA((3,)),
-            pltpu.SemaphoreType.DMA((2,)),
-            pltpu.SemaphoreType.DMA,
-            pltpu.SemaphoreType.DMA((4,)),
-        ],
-        compiler_params=params(1),
-        cost_estimate=pl.CostEstimate(flops=1 << 28, bytes_accessed=2 << 20, transcendentals=0),
-        name="cross_attention",
-    )(source_lengths, target_lengths, states, moe, upstream[0], attention_gain, final)
-    gate_grad, input_grad = pl.pallas_call(
-        backward_kernel,
-        out_shape=(shape((TOK, 2), F32), shape((TOK, D), BF)),
-        in_specs=[VM] * 6 + [HB] * 3,
-        out_specs=(VM, VM),
-        scratch_shapes=[
-            pltpu.VMEM((D, D), BF),
-            pltpu.VMEM((D, D), BF),
-            pltpu.VMEM((4, BLOCK, D), BF),
-            pltpu.VMEM((BLOCK, D), BF),
-            pltpu.VMEM((BLOCK, D), BF),
-            pltpu.VMEM((BLOCK, D), BF),
-            pltpu.VMEM((PACKED, 128), BF),
-            pltpu.VMEM((128, PACKED), BF),
-            pltpu.SemaphoreType.DMA((3,)),
-        ]
-        + Exchange.scratch,
-        compiler_params=params(2),
-        cost_estimate=pl.CostEstimate(flops=flops, bytes_accessed=8 << 20, transcendentals=0),
-        name="moe_backward",
-    )(x, moe_up, ids, gates, mixture_gain, back, expert_in[0], expert_out[0], hidden)
-    return (gate_grad[None], input_grad[None])
+        cost_estimate=pl.CostEstimate(
+            flops=8 * 1024 * 1024 * 1024, bytes_accessed=8 << 20, transcendentals=0
+        ),
+        name="mixture_step",
+    )(
+        source_lengths,
+        target_lengths,
+        layer_in[0],
+        upstream[0],
+        expert_ids[0].T,
+        gate_values[0].T,
+        attention_gain,
+        mixture_gain,
+        final_gain.reshape(1, D),
+        expert_in[0],
+        expert_out[0],
+    )
+    return (gate_grad.T[None], input_grad[None])
 
 
 def solution(mesh):

time: 209 us -> 189 us (0.904)
  the two profiles are of different devices: /device:TPU:32 before, /device:TPU:2 now
where the time goes in v3:
time: 189 us
  Pallas kernels  184 us (97%)
  local copies, waits for them, and re-layouts  2.9 us (2%)
  between operations  1.93 us (1%)
    pallas_call x1, Pallas kernels, body(): pl.pallas_call(whole_kernel, out_shape=(shape((2, TOK), F32), shape((TOK,...  184 us

profile of v3, /device:TPU:2, one launch (start us, length us, event | category | flops | bytes accessed | tf_op | source)
XLA Modules:
  0.0 188.9 jit_solution(13759835344512272963)
XLA Ops:
  1.9 184.1 %mixture_step.1 = (f32[2,128]{1,0:T(2,128)}, bf16[128,1024]{1,0:T(8,128)(2,1)}) custom-call(s32[1]{0:T(128)S(6)} %copy.15.source_len, s32[1]{0:T(128)S(6)} %copy.16.target_len, bf16[128,1024]{1,0:T(8,128)(2,1)} %bitcast.19, bf16[128,1024]{1,0:T(8,128)(2,1)} %bitcast.20, s32[2,128]{1,0:T(2,128)} %bitcast.22, f32[2,128]{1,0:T(2,128)} %bitcast.23, ...), custom_call_target="tpu_custom_call" | custom-call | flops 8589934592 | bytes 8388608 | tf_op jit(solution)/shard_map/mixture_step/pallas_call | solution.py:821
  186.0 1.2 copy.17
  187.2 1.7 copy.18

commit v4 on v3

--- a/solution.py
+++ b/solution.py
@@ -421,10 +421,15 @@
     pltpu.VMEM((TOK, 256), BF),
     pltpu.VMEM((4, TOK, 256), BF),
     pltpu.VMEM((TOK, 256), F32),
-    pltpu.SemaphoreType.DMA((10,)),
+    pltpu.VMEM((TOK, 256), BF),
+    pltpu.VMEM((4, TOK, 256), BF),
+    pltpu.SemaphoreType.DMA((12,)),
     pltpu.SemaphoreType.DMA((4,)),
     pltpu.SemaphoreType.DMA((4,)),
     pltpu.SemaphoreType.DMA((3,)),
+    pltpu.SemaphoreType.DMA((2,)),
+    pltpu.SemaphoreType.DMA,
+    pltpu.SemaphoreType.DMA((4,)),
     pltpu.SemaphoreType.DMA((2,)),
     pltpu.SemaphoreType.DMA,
     pltpu.SemaphoreType.DMA((4,)),
@@ -448,6 +453,8 @@
     final_out,
     final_in,
     total,
+    relayed,
+    far_in,
     s_send,
     s_recv,
     t_send,
@@ -455,43 +462,65 @@
     x_sem,
     f_send,
     f_recv,
+    y_sem,
+    r_send,
+    r_recv,
 ):
     s = lax.axis_index("section")
     p = lax.axis_index("expert")
+    side = p + 2 - 4 * ((p // 2) % 2)
     x = s % 4
     low_z = s < 4
     high_z = s >= 4
     bridge = s == 1
     decoder = s >= 2
     low_decoder = jnp.logical_and(low_z, decoder)
-    relay = jnp.logical_and(low_z, s != 1)
-
-    first_sends = [(0, 0), (2, 2), (3, 3), (1, 5)]
-    later_sends = [(0, 2), (1, 2), (3, 2), (0, 3), (1, 3), (2, 3)]
-    sends = first_sends + later_sends
-
-    def bridge_copy(i):
-        quarter, target = sends[i]
+    sender = jnp.logical_and(low_z, s != 1)
+
+    relays = (0, 2, 3, 1)
+    direct = ((2, 2), (3, 3), (3, 2), (0, 3), (0, 2), (1, 3), (1, 2), (2, 3))
+
+    def relay_copy(i):
         return remote(
-            states_ref.at[quarter], held.at[quarter], s_send.at[i], s_recv.at[quarter], target, p
-        )
+            states_ref.at[relays[i]], relayed, s_send.at[i], y_sem.at[1], relays[i], side
+        )
+
+    def direct_copy(i):
+        quarter, target = direct[i]
+        return remote(
+            states_ref.at[quarter],
+            held.at[quarter],
+            s_send.at[4 + i],
+            s_recv.at[quarter],
+            target,
+            p,
+        )
+
+    def relay_on():
+        return remote(relayed, held.at[x], y_sem.at[0], s_recv.at[x], x + 4, side)
 
     def onward(slot, target):
         return remote(held.at[x], held.at[x], s_send.at[slot], s_recv.at[x], target, p)
 
     def arrived(quarter):
         onto = held.at[quarter]
-        return remote(onto, onto, s_send.at[0], s_recv.at[quarter], s, p)
+        return remote(onto, onto, s_send.at[0], s_recv.at[quarter], s, side)
 
     @pl.when(bridge)
     def _():
-        for i in range(len(sends)):
-            bridge_copy(i).start()
-
-    @pl.when(relay)
+        for i in range(len(relays)):
+            relay_copy(i).start()
+        for i in range(len(direct)):
+            direct_copy(i).start()
+
+    @pl.when(low_z)
+    def _():
+        remote(relayed, relayed, y_sem.at[0], y_sem.at[1], s, side).wait_recv()
+        relay_on().start()
+
+    @pl.when(low_decoder)
     def _():
         arrived(x).wait_recv()
-        onward(0, x + 4).start()
 
     @pl.when(high_z)
     def _():
@@ -510,7 +539,7 @@
         )
 
     def term_in(slot):
-        return remote(terms.at[0], terms_in.at[slot], t_send.at[0], t_recv.at[slot], s, p)
+        return remote(terms.at[0], terms_in.at[slot], t_send.at[0], t_recv.at[slot], s, side)
 
     @pl.when(decoder)
     def _():
@@ -562,14 +591,20 @@
                 def _():
                     term_low(k).start()
 
-    def cross_copy(target):
-        return remote(cross_out, cross_in, x_sem.at[0], x_sem.at[1], target, p)
+    def cross_copy():
+        return remote(cross_out, cross_in, x_sem.at[0], x_sem.at[1], x, side)
 
     def final_copy():
         return remote(final_out, final_in.at[x], f_send, f_recv.at[x], 1, p)
 
     def final_arrived(quarter):
-        return remote(final_out, final_in.at[quarter], f_send, f_recv.at[quarter], s, p)
+        return remote(final_out, final_in.at[quarter], f_send, f_recv.at[quarter], s, side)
+
+    def far_copy():
+        return remote(cross_in, far_in.at[x], r_send, r_recv.at[x], 1, side)
+
+    def far_arrived(quarter):
+        return remote(cross_in, far_in.at[quarter], r_send, r_recv.at[quarter], s, side)
 
     @pl.when(high_z)
     def _():
@@ -579,8 +614,7 @@
         for slot in range(3):
             summed = summed + terms_in[slot].astype(F32)
         cross_out[...] = summed.astype(BF)
-        cross_copy(x).start()
-        cross_copy(x).wait_send()
+        cross_copy().start()
 
     @pl.when(s < 2)
     def _():
@@ -595,14 +629,15 @@
                 term_in(slot).wait_recv()
                 total[...] += terms_in[slot].astype(F32)
 
-        cross_copy(s).wait_recv()
-        total[...] += cross_in[...].astype(F32)
-
-    @pl.when(relay)
+    @pl.when(sender)
     def _():
         final_out[...] = total[...].astype(BF)
         final_copy().start()
-        final_copy().wait_send()
+
+    @pl.when(low_z)
+    def _():
+        remote(cross_in, cross_in, x_sem.at[0], x_sem.at[1], s, side).wait_recv()
+        far_copy().start()
 
     @pl.when(s == 0)
     def _():
@@ -613,30 +648,46 @@
         pieces = []
         for quarter in range(4):
             if quarter == 1:
-                pieces.append(total[...])
+                near = total[...]
             else:
                 final_arrived(quarter).wait_recv()
-                pieces.append(final_in[quarter].astype(F32))
+                near = final_in[quarter].astype(F32)
+            far_arrived(quarter).wait_recv()
+            pieces.append(near + far_in[quarter].astype(F32))
         cotangent = jnp.concatenate(pieces, axis=1)
         v = moe_ref[...].astype(F32)
         up_ref[...] = rms_back(v, final_ref[...], cotangent).astype(BF)
-        for i in range(len(sends)):
-            bridge_copy(i).wait_send()
-
-    @pl.when(relay)
-    def _():
-        onward(0, x + 4).wait_send()
-
-    @pl.when(high_z)
-    def _():
-        for d in range(1, 4):
-            onward(d, 4 + (x + d) % 4).wait_send()
-            term_high(d).wait_send()
-
-    @pl.when(low_decoder)
-    def _():
-        for d in range(1, 4):
-            term_low(d).wait_send()
+
+    def finish():
+        @pl.when(bridge)
+        def _():
+            for i in range(len(relays)):
+                relay_copy(i).wait_send()
+            for i in range(len(direct)):
+                direct_copy(i).wait_send()
+
+        @pl.when(low_z)
+        def _():
+            relay_on().wait_send()
+            far_copy().wait_send()
+
+        @pl.when(sender)
+        def _():
+            final_copy().wait_send()
+
+        @pl.when(high_z)
+        def _():
+            cross_copy().wait_send()
+            for d in range(1, 4):
+                onward(d, 4 + (x + d) % 4).wait_send()
+                term_high(d).wait_send()
+
+        @pl.when(low_decoder)
+        def _():
+            for d in range(1, 4):
+                term_low(d).wait_send()
+
+    return finish
 
 
 def whole_kernel(
@@ -681,7 +732,10 @@
     p = lax.axis_index("expert")
     ahead.greet()
     for d in range(1, 8):
-        pl.semaphore_signal(barrier, inc=1, device_id=((s + d) % 8, p), device_id_type=MESH)
+        for other in (p, ahead.pair_partner()):
+            pl.semaphore_signal(
+                barrier, inc=1, device_id=((s + d) % 8, other), device_id_type=MESH
+            )
     in_copy.start()
     out_copy.start()
 
@@ -692,7 +746,7 @@
     packing[...] = pack_matrix()
     slots = pack(dot(placing_t, normed).astype(BF), packing[...])
     ahead.slots[...] = slots.reshape(EXPERTS, PAD, PACKED)
-    pl.semaphore_wait(barrier, 39)
+    pl.semaphore_wait(barrier, 46)
     ahead.send_out()
     matches[0] = first.astype(BF)
     matches[1] = second.astype(BF)
@@ -735,7 +789,7 @@
         for quarter in range(4):
             states_ref[quarter] = states[:, quarter * 256 : (quarter + 1) * 256]
 
-    cross_part(
+    finish_cross = cross_part(
         source_len,
         target_len,
         states_ref,
@@ -786,6 +840,7 @@
     back = rms_back(x_ref[...].astype(F32), mixture_ref[...], normed_grad)
     grad_ref[...] = (up_ref[...].astype(F32) + back).astype(BF)
     ahead.finish()
+    finish_cross()
     behind.finish()
 
 

time: 189 us -> 194 us (1.026)
  the two profiles are of different devices: /device:TPU:2 before, /device:TPU:10 now
where the time goes in v4:
time: 194 us
  Pallas kernels  189 us (97%)
  local copies, waits for them, and re-layouts  2.9 us (1%)
    pallas_call x1, Pallas kernels, body(): pl.pallas_call(whole_kernel, out_shape=(shape((2, TOK), F32), shape((TOK,...  189 us

profile of v4, /device:TPU:10, one launch (start us, length us, event | category | flops | bytes accessed | tf_op | source)
XLA Modules:
  0.0 194.0 jit_solution(13574506357524083982)
XLA Ops:
  1.9 189.2 %mixture_step.1 = (f32[2,128]{1,0:T(2,128)}, bf16[128,1024]{1,0:T(8,128)(2,1)}) custom-call(s32[1]{0:T(128)S(6)} %copy.15.source_len, s32[1]{0:T(128)S(6)} %copy.16.target_len, bf16[128,1024]{1,0:T(8,128)(2,1)} %bitcast.19, bf16[128,1024]{1,0:T(8,128)(2,1)} %bitcast.20, s32[2,128]{1,0:T(2,128)} %bitcast.22, f32[2,128]{1,0:T(2,128)} %bitcast.23, ...), custom_call_target="tpu_custom_call" | custom-call | flops 8589934592 | bytes 8388608 | tf_op jit(solution)/shard_map/mixture_step/pallas_call | solution.py:876
  191.1 1.2 copy.17
  192.4 1.7 copy.18

commit v5 on v3

--- a/solution.py
+++ b/solution.py
@@ -138,15 +138,15 @@
         pltpu.VMEM((4, 2, 2, 4, PAD, PACKED), BF),
         pltpu.VMEM((4, 2, 2, 4, PAD, PACKED), BF),
         pltpu.VMEM((4, 2, 4, PAD, PACKED), BF),
-        pltpu.VMEM((4, 2, 4, PAD, PACKED), BF),
-        pltpu.VMEM((4, 2, 4, PAD, PACKED), BF),
-        pltpu.VMEM((4, 2, 4, PAD, PACKED), BF),
+        pltpu.VMEM((4, 4, PAD, PACKED), BF),
+        pltpu.VMEM((4, 4, PAD, PACKED), BF),
+        pltpu.VMEM((4, 4, PAD, PACKED), BF),
         pltpu.VMEM((EXPERTS, PAD, PACKED), BF),
         pltpu.SemaphoreType.DMA((4, 4)),
-        pltpu.SemaphoreType.DMA((4, 2, 4)),
         pltpu.SemaphoreType.DMA((4, 4)),
+        pltpu.SemaphoreType.DMA((5, 4)),
+        pltpu.SemaphoreType.DMA((5, 4)),
         pltpu.SemaphoreType.DMA((4, 4)),
-        pltpu.SemaphoreType.DMA((4, 2, 4)),
         pltpu.SemaphoreType.DMA((4, 4)),
     ]
 
@@ -186,102 +186,75 @@
 
     def greet(self):
         barrier = pltpu.get_barrier_semaphore()
-
-        def signal(other):
+        for dz in range(4):
+            for dy in range(4):
+                if dz or dy:
+                    other = self.device(
+                        (self.ey + dy) % 4, (self.ez + dz) % 4, self.half, self.core
+                    )
+                    pl.semaphore_signal(
+                        barrier, inc=1, device_id=(self.section, other), device_id_type=MESH
+                    )
+        for other in (self.core_partner(), self.pair_partner()):
             pl.semaphore_signal(
                 barrier, inc=1, device_id=(self.section, other), device_id_type=MESH
             )
 
-        for dz in range(4):
-            for dy in range(4):
-                for dh in range(2):
-                    if dz or dy or dh:
-                        signal(
-                            self.device(
-                                (self.ey + dy) % 4,
-                                (self.ez + dz) % 4,
-                                (self.half + dh) % 2,
-                                self.core,
-                            )
-                        )
-        signal(self.core_partner())
-
-    def source(self, t):
-        return (self.ez + 4 - SHIFTS[t]) % 4
-
-    def near(self, t):
-        return 1 - (self.ez + 4 - SHIFTS[t]) // 4
-
-    def far(self, t):
-        return [dy for dy in range(4) if SHIFTS[t] or dy]
-
-    def copy(self, src, dst, send, recv, target):
-        return remote(src, dst, send, recv, self.section, target)
-
     def out_copy(self, t, dy):
         ey, ez = (self.ey + dy) % 4, (self.ez + SHIFTS[t]) % 4
-        half = (self.ez + SHIFTS[t]) // 4 if SHIFTS[t] else self.half
-        return self.copy(
+        return remote(
             self.slots.at[ey * 4 + ez],
             self.rows.at[self.ez, self.core, self.half, self.ey],
             self.a_send.at[t, dy],
-            self.a_recv.at[t, self.half, dy],
-            self.device(ey, ez, half, self.core),
-        )
-
-    def out_arrival(self, t, half, dy):
-        block = self.rows.at[self.source(t), self.core, half, (self.ey + 4 - dy) % 4]
-        return self.copy(
-            block, block, self.a_send.at[t, dy], self.a_recv.at[t, half, dy], self.core_partner()
-        )
-
-    def pair_share(self, t, half=None):
-        block = self.rows.at[self.source(t), self.core]
-        if half is not None:
-            block = block.at[half]
-        return self.copy(
-            block, block, self.g_send.at[0, t], self.g_recv.at[0, t], self.pair_partner()
-        )
-
-    def core_share(self, t):
-        block = self.rows.at[self.source(t), self.core]
-        return self.copy(
-            block, block, self.g_send.at[1, t], self.g_recv.at[1, t], self.core_partner()
+            self.a_recv.at[t, dy],
+            self.section,
+            self.device(ey, ez, self.half, self.core),
+        )
+
+    def source(self, t):
+        return (self.ez + 4 - SHIFTS[t]) % 4
+
+    def piece(self, t, kind):
+        half = self.half if kind < 2 else 1 - self.half
+        ref = self.rows.at[self.source(t), self.core, half]
+        target = self.pair_partner() if kind == 0 else self.core_partner()
+        return remote(
+            ref, ref, self.g_send.at[kind, t], self.g_recv.at[kind, t], self.section, target
         )
 
     def core_copy(self, t):
-        return self.copy(
+        return remote(
             self.products.at[t, 1 - self.core],
             self.core_part.at[t],
-            self.g_send.at[2, t],
-            self.g_recv.at[2, t],
+            self.g_send.at[3, t],
+            self.g_recv.at[3, t],
+            self.section,
             self.core_partner(),
         )
 
-    def pair_copy(self, t, half=None):
-        src, dst = self.pair_out.at[t], self.pair_in.at[t]
-        if half is not None:
-            src, dst = src.at[half], dst.at[half]
-        return self.copy(
-            src, dst, self.g_send.at[3, t], self.g_recv.at[3, t], self.pair_partner()
-        )
-
-    def back_copy(self, t, half, dy):
+    def pair_copy(self, t):
+        return remote(
+            self.pair_out.at[t],
+            self.pair_in.at[t],
+            self.g_send.at[4, t],
+            self.g_recv.at[4, t],
+            self.section,
+            self.pair_partner(),
+        )
+
+    def back_copy(self, t, dy):
         ey = (self.ey + 4 - dy) % 4
-        return self.copy(
-            self.sums.at[t, half, ey],
+        return remote(
+            self.sums.at[t, ey],
             self.back.at[self.mine],
-            self.f_send.at[t, half, dy],
+            self.f_send.at[t, dy],
             self.f_recv.at[t, dy],
-            self.device(ey, self.source(t), half, self.core),
-        )
-
-    def back_arrival(self, t, dy):
-        ey, ez = (self.ey + dy) % 4, (self.ez + SHIFTS[t]) % 4
-        block = self.back.at[ey * 4 + ez]
-        return self.copy(
-            block, block, self.f_send.at[t, 0, dy], self.f_recv.at[t, dy], self.core_partner()
-        )
+            self.section,
+            self.device(ey, self.source(t), self.half, self.core),
+        )
+
+    def far(self, t):
+        return [dy for dy in range(4) if SHIFTS[t] or dy]
 
     def send_out(self):
         for t in range(4):
@@ -290,78 +263,42 @@
         self.rows[self.ez, self.core, self.half, self.ey] = self.slots[self.mine]
 
     def share(self, t):
-        if SHIFTS[t] == 0:
-            for dy in self.far(t):
-                self.out_arrival(t, self.half, dy).wait_recv()
-            self.pair_share(t, self.half).start()
-            return
-
-        @pl.when(self.half == self.near(t))
-        def _():
-            for half in range(2):
-                for dy in self.far(t):
-                    self.out_arrival(t, half, dy).wait_recv()
-            self.pair_share(t).start()
-            self.core_share(t).start()
+        for dy in self.far(t):
+            self.out_copy(t, dy).wait_recv()
+        self.piece(t, 0).start()
+        self.piece(t, 1).start()
 
     def pass_on(self, t):
-        if SHIFTS[t] == 0:
-            self.pair_share(t, 1 - self.half).wait_recv()
-            self.core_share(t).start()
-            return
-
-        @pl.when(self.half != self.near(t))
-        def _():
-            self.pair_share(t).wait_recv()
-            self.core_share(t).start()
+        self.piece(t, 0).wait_recv()
+        self.piece(t, 2).start()
 
     def multiply(self, t, experts):
-        self.core_share(t).wait_recv()
+        self.piece(t, 1).wait_recv()
+        self.piece(t, 2).wait_recv()
         experts(t, self.source(t))
         self.core_copy(t).start()
 
     def core_sum(self, t):
         self.core_copy(t).wait_recv()
+        other = 1 - self.half
+        total = self.products[t, self.core, other].astype(F32) + self.core_part[t, other].astype(
+            F32
+        )
+        self.pair_out[t] = total.astype(BF)
+        self.pair_copy(t).start()
+
+    def pair_sum(self, t):
+        self.pair_copy(t).wait_recv()
+        total = (
+            self.products[t, self.core, self.half].astype(F32)
+            + self.core_part[t, self.half].astype(F32)
+            + self.pair_in[t].astype(F32)
+        )
+        self.sums[t] = total.astype(BF)
+        for dy in self.far(t):
+            self.back_copy(t, dy).start()
         if SHIFTS[t] == 0:
-            other = 1 - self.half
-            self.pair_out[t, other] = (
-                self.products[t, self.core, other].astype(F32)
-                + self.core_part[t, other].astype(F32)
-            ).astype(BF)
-            self.pair_copy(t, other).start()
-            return
-
-        @pl.when(self.half != self.near(t))
-        def _():
-            self.pair_out[t] = (
-                self.products[t, self.core].astype(F32) + self.core_part[t].astype(F32)
-            ).astype(BF)
-            self.pair_copy(t).start()
-
-    def pair_sum(self, t):
-        if SHIFTS[t] == 0:
-            self.pair_copy(t, self.half).wait_recv()
-            self.sums[t, self.half] = (
-                self.products[t, self.core, self.half].astype(F32)
-                + self.core_part[t, self.half].astype(F32)
-                + self.pair_in[t, self.half].astype(F32)
-            ).astype(BF)
-            for dy in self.far(t):
-                self.back_copy(t, self.half, dy).start()
-            self.back[self.mine] = self.sums[t, self.half, self.ey]
-            return
-
-        @pl.when(self.half == self.near(t))
-        def _():
-            self.pair_copy(t).wait_recv()
-            self.sums[t] = (
-                self.products[t, self.core].astype(F32)
-                + self.core_part[t].astype(F32)
-                + self.pair_in[t].astype(F32)
-            ).astype(BF)
-            for half in range(2):
-                for dy in self.far(t):
-                    self.back_copy(t, half, dy).start()
+            self.back[self.mine] = self.sums[t, self.ey]
 
     def run(self, experts):
         for step in range(8):
@@ -376,31 +313,17 @@
                     stage(step - lag)
         for t in range(4):
             for dy in self.far(t):
-                self.back_arrival(t, dy).wait_recv()
+                self.back_copy(t, dy).wait_recv()
 
     def finish(self):
         for t in range(4):
             for dy in self.far(t):
                 self.out_copy(t, dy).wait_send()
-            self.core_share(t).wait_send()
+                self.back_copy(t, dy).wait_send()
+            for kind in range(3):
+                self.piece(t, kind).wait_send()
             self.core_copy(t).wait_send()
-            if SHIFTS[t] == 0:
-                self.pair_share(t, self.half).wait_send()
-                self.pair_copy(t, 1 - self.half).wait_send()
-                for dy in self.far(t):
-                    self.back_copy(t, self.half, dy).wait_send()
-                continue
-
-            @pl.when(self.half == self.near(t))
-            def _():
-                self.pair_share(t).wait_send()
-                for half in range(2):
-                    for dy in self.far(t):
-                        self.back_copy(t, half, dy).wait_send()
-
-            @pl.when(self.half != self.near(t))
-            def _():
-                self.pair_copy(t).wait_send()
+            self.pair_copy(t).wait_send()
 
     def received(self, t, full, matrix):
         packed = self.rows[self.source(t)].reshape(BLOCK, PACKED)
@@ -692,7 +615,7 @@
     packing[...] = pack_matrix()
     slots = pack(dot(placing_t, normed).astype(BF), packing[...])
     ahead.slots[...] = slots.reshape(EXPERTS, PAD, PACKED)
-    pl.semaphore_wait(barrier, 39)
+    pl.semaphore_wait(barrier, 24)
     ahead.send_out()
     matches[0] = first.astype(BF)
     matches[1] = second.astype(BF)

time: 189 us -> 187 us (0.989)
  the two profiles are of different devices: /device:TPU:2 before, /device:TPU:34 now
where the time goes in v5:
time: 187 us
  Pallas kernels  182 us (97%)
  local copies, waits for them, and re-layouts  2.9 us (2%)
  between operations  1.93 us (1%)
    pallas_call x1, Pallas kernels, body(): pl.pallas_call(whole_kernel, out_shape=(shape((2, TOK), F32), shape((TOK,...  182 us

profile of v5, /device:TPU:34, one launch (start us, length us, event | category | flops | bytes accessed | tf_op | source)
XLA Modules:
  0.0 186.6 jit_solution(5200991594678491549)
XLA Ops:
  1.9 181.8 %mixture_step.1 = (f32[2,128]{1,0:T(2,128)}, bf16[128,1024]{1,0:T(8,128)(2,1)}) custom-call(s32[1]{0:T(128)S(6)} %copy.15.source_len, s32[1]{0:T(128)S(6)} %copy.16.target_len, bf16[128,1024]{1,0:T(8,128)(2,1)} %bitcast.19, bf16[128,1024]{1,0:T(8,128)(2,1)} %bitcast.20, s32[2,128]{1,0:T(2,128)} %bitcast.22, f32[2,128]{1,0:T(2,128)} %bitcast.23, ...), custom_call_target="tpu_custom_call" | custom-call | flops 8589934592 | bytes 8388608 | tf_op jit(solution)/shard_map/mixture_step/pallas_call | solution.py:744
  183.7 1.2 copy.17
  184.9 1.7 copy.18

commit v6 on v5

--- a/solution.py
+++ b/solution.py
@@ -20,7 +20,7 @@
 PACKED = 896
 ROWS = EXPERTS * PAD
 BLOCK = ROWS
-TILE = 256
+TILE = 512
 SHIFTS = (2, 3, 1, 0)
 NT = (((1,), (1,)), ((), ()))
 
@@ -301,16 +301,33 @@
             self.back[self.mine] = self.sums[t, self.ey]
 
     def run(self, experts):
-        for step in range(8):
-            for stage, lag in (
-                (self.share, 0),
-                (self.pass_on, 1),
-                (lambda t: self.multiply(t, experts), 2),
-                (self.core_sum, 3),
-                (self.pair_sum, 4),
-            ):
-                if 0 <= step - lag < 4:
-                    stage(step - lag)
+        def multiply(t):
+            self.multiply(t, experts)
+
+        share, pass_on, core_sum, pair_sum = self.share, self.pass_on, self.core_sum, self.pair_sum
+        for stage, t in (
+            (share, 0),
+            (share, 3),
+            (share, 1),
+            (pass_on, 0),
+            (share, 2),
+            (pass_on, 1),
+            (pass_on, 3),
+            (multiply, 0),
+            (pass_on, 2),
+            (multiply, 1),
+            (core_sum, 0),
+            (multiply, 2),
+            (core_sum, 1),
+            (pair_sum, 0),
+            (multiply, 3),
+            (core_sum, 2),
+            (pair_sum, 1),
+            (core_sum, 3),
+            (pair_sum, 2),
+            (pair_sum, 3),
+        ):
+            stage(t)
         for t in range(4):
             for dy in self.far(t):
                 self.back_copy(t, dy).wait_recv()
@@ -586,6 +603,7 @@
     unpacking,
     matches,
     weights,
+    turned,
     moe_ref,
     states_ref,
     summed_ref,
@@ -620,6 +638,7 @@
     matches[0] = first.astype(BF)
     matches[1] = second.astype(BF)
     weights[...] = weighted
+    turned[0], turned[1] = split(weighted.T)
     unpacking[...] = unpack_matrix()
     in_copy.wait()
     out_copy.wait()
@@ -671,8 +690,7 @@
     )
 
     up_low = up_ref[...]
-    high, low = split(weights[...].T)
-    grads = dot(high, up_low) + dot(low, up_low)
+    grads = dot(turned[0], up_low) + dot(turned[1], up_low)
     behind.slots[...] = pack(grads.astype(BF), packing[...]).reshape(EXPERTS, PAD, PACKED)
     behind.send_out()
     wide_up = up_low.astype(F32)
@@ -757,6 +775,7 @@
             vmem((128, PACKED), BF),
             vmem((2, TOK, ROWS), BF),
             vmem((TOK, ROWS), F32),
+            vmem((2, ROWS, TOK), BF),
             vmem((TOK, D), BF),
             vmem((4, TOK, 256), BF),
             vmem((ROWS, D), BF),

time: 187 us -> 183 us (0.979)
  the two profiles are of different devices: /device:TPU:34 before, /device:TPU:98 now
where the time goes in v6:
time: 183 us
  Pallas kernels  178 us (97%)
  local copies, waits for them, and re-layouts  2.9 us (2%)
  between operations  1.93 us (1%)
    pallas_call x1, Pallas kernels, body(): pl.pallas_call(whole_kernel, out_shape=(shape((2, TOK), F32), shape((TOK,...  178 us

profile of v6, /device:TPU:98, one launch (start us, length us, event | category | flops | bytes accessed | tf_op | source)
XLA Modules:
  0.0 182.6 jit_solution(4751756310877360950)
XLA Ops:
  1.9 177.8 %mixture_step.1 = (f32[2,128]{1,0:T(2,128)}, bf16[128,1024]{1,0:T(8,128)(2,1)}) custom-call(s32[1]{0:T(128)S(6)} %copy.15.source_len, s32[1]{0:T(128)S(6)} %copy.16.target_len, bf16[128,1024]{1,0:T(8,128)(2,1)} %bitcast.19, bf16[128,1024]{1,0:T(8,128)(2,1)} %bitcast.20, s32[2,128]{1,0:T(2,128)} %bitcast.22, f32[2,128]{1,0:T(2,128)} %bitcast.23, ...), custom_call_target="tpu_custom_call" | custom-call | flops 8589934592 | bytes 8388608 | tf_op jit(solution)/shard_map/mixture_step/pallas_call | solution.py:762
  179.7 1.2 copy.17
  181.0 1.7 copy.18
